TPU v7x, 32 devices: a whole 2x2x4 slice. The times are simulated.
32 devices in a mesh: dp: 8 (over z, x), ctx: 4 (over y, core).
Axes of the slice: x: 2, y: 2, z: 4, core: 2. Of those that a mesh axis runs over, the one named last changes fastest.
Arguments:
- block_input: bfloat16 [8, 2048, 2048], P('dp', 'ctx'), may hold values from -6 to 6
- segment_ids: int32 [8, 2048], P('dp', 'ctx'), may hold values from 0 to 5, never falling along the last dimension, each value on 1 to 800 neighbouring positions
- cotangent: bfloat16 [8, 2048, 2048], P('dp', 'ctx'), may hold values from -6 to 6
- in_weight: float32 [2048, 8240], P(('dp', 'ctx')), may hold values from -0.125 to 0.125
- out_weight: float32 [4096, 2048], P(('dp', 'ctx')), may hold values from -0.375 to 0.375
- gate_up_weight: float32 [2048, 8192], P(('dp', 'ctx')), may hold values from -0.125 to 0.125
- down_weight: float32 [4096, 2048], P(('dp', 'ctx')), may hold values from -0.09375 to 0.09375
- in_first: float32 [2048, 8240], P(('dp', 'ctx')), may hold values from -40 to 40
- out_first: float32 [4096, 2048], P(('dp', 'ctx')), may hold values from -40 to 40
- gate_up_first: float32 [2048, 8192], P(('dp', 'ctx')), may hold values from -40 to 40
- down_first: float32 [4096, 2048], P(('dp', 'ctx')), may hold values from -40 to 40
- in_second: float32 [2048, 8240], P(('dp', 'ctx')), may hold values from 212.992 to 868.352
- out_second: float32 [4096, 2048], P(('dp', 'ctx')), may hold values from 212.992 to 868.352
- gate_up_second: float32 [2048, 8192], P(('dp', 'ctx')), may hold values from 212.992 to 868.352
- down_second: float32 [4096, 2048], P(('dp', 'ctx')), may hold values from 212.992 to 868.352
- small_params: float32 [7312], replicated, may hold values from -5 to 1.5
- small_first: float32 [7312], replicated, may hold values from -80 to 80
- small_second: float32 [7312], replicated, may hold values from 819.2 to 3276.8
Outputs:
- block_output: bfloat16 [8, 2048, 2048], P('dp', 'ctx')
- input_grad: float32 [8, 2048, 2048], P('dp', 'ctx')
- new_in_weight: float32 [2048, 8240], P(('dp', 'ctx'))
- new_in_first: float32 [2048, 8240], P(('dp', 'ctx'))
- new_in_second: float32 [2048, 8240], P(('dp', 'ctx'))
- new_out_weight: float32 [4096, 2048], P(('dp', 'ctx'))
- new_out_first: float32 [4096, 2048], P(('dp', 'ctx'))
- new_out_second: float32 [4096, 2048], P(('dp', 'ctx'))
- new_gate_up_weight: float32 [2048, 8192], P(('dp', 'ctx'))
- new_gate_up_first: float32 [2048, 8192], P(('dp', 'ctx'))
- new_gate_up_second: float32 [2048, 8192], P(('dp', 'ctx'))
- new_down_weight: float32 [4096, 2048], P(('dp', 'ctx'))
- new_down_first: float32 [4096, 2048], P(('dp', 'ctx'))
- new_down_second: float32 [4096, 2048], P(('dp', 'ctx'))
- new_small_params: float32 [7312], replicated
- new_small_first: float32 [7312], replicated
- new_small_second: float32 [7312], replicated
All inputs are finite; a program needn't handle non-finite values.
Results may differ from a plain program's by a relative error of at most 0.013.
The roundings to bfloat16 on the way count: a program that leaves them out, or rounds other values in their place, can miss the bound.
Values may be sent and summed in bfloat16 or wider, within the bound.
No kernel may reach another device: no remote copies, remote signals or barrier semaphores. Data moves between devices by JAX's collectives and lax.ppermute only.
A program may use at most 576 MiB of HBM per device.

v0:
```python
import functools
import math

import jax
import jax.numpy as jnp
from jax import lax
from jax.experimental import pallas as pl
from jax.experimental.pallas import tpu as pltpu
from jax.sharding import PartitionSpec as P

D = 2048
FF = 4096
QH = 8
KVH = 2
HD = 128
HEADS_M = 48
HEAD_M = 64
STATE = 256
STEP = 10
DOC_MOST = 800
DSSM = HEADS_M * HEAD_M
SHARED = 2 * STATE + 2 * KVH * HD + 128
CHUNK = 256
QBLOCK = 256

norm_eps = 1e-05
beta_one = 0.9
beta_two = 0.95
adam_eps = 1e-08
weight_decay = 0.1
rate_scale = 3.0
small_rate = 0.3
bf16 = jnp.bfloat16
f32 = jnp.float32
NN = (((1,), (0,)), ((), ()))
NT = (((1,), (1,)), ((), ()))
TN = (((0,), (0,)), ((), ()))


def dot(a, b, dims=NN):
    return lax.dot_general(a, b, dims, preferred_element_type=f32)


def from_ctx(x, m):
    count = lax.axis_size("ctx")
    return lax.ppermute(x, "ctx", [(i ^ m, i) for i in range(count)])


def from_dp(x, j, k):
    count = lax.axis_size("dp")
    inner = count // 4
    pairs = []
    for i in range(count):
        z, w = divmod(i, inner)
        pairs.append((((z + j) % 4) * inner + (w + k) % inner, i))
    return lax.ppermute(x, "dp", pairs)


def fence(*trees):
    return lax.optimization_barrier(trees)


def outer_groups():
    count = lax.axis_size("dp")
    inner = count // 4
    return [[j * inner + k for j in range(4)] for k in range(inner)]


def gather_outer(own):
    return lax.all_gather(own, "dp", axis_index_groups=outer_groups())


def gather_outer_permuted(own):
    outer = lax.axis_index("dp") // (lax.axis_size("dp") // 4)
    full = jnp.stack([own] * 4)
    for j in (1, 3, 2):
        full = lax.dynamic_update_index_in_dim(
            full, from_dp(own, j, 0), lax.rem(outer + j, 4), 0
        )
    return full


def gather_inner(along):
    return {k: from_dp(along, 0, k) for k in range(1, lax.axis_size("dp") // 4)}


def place_dp(along, others):
    inner = lax.axis_size("dp") // 4
    place = lax.rem(lax.axis_index("dp"), inner)
    full = jnp.stack([along] * inner, axis=1)
    for k, block in others.items():
        full = lax.dynamic_update_index_in_dim(full, block, lax.rem(place + k, inner), 1)
    return full


def scatter_inner(full):
    inner = lax.axis_size("dp") // 4
    place = lax.rem(lax.axis_index("dp"), inner)
    full = full.reshape((4, inner) + full.shape[1:])

    def part(k):
        return lax.dynamic_index_in_dim(full, lax.rem(place + k, inner), 1, False)

    return part(0), {k: from_dp(part(k), 0, -k) for k in range(1, inner)}


def scatter_outer(own, got):
    total = own.astype(f32)
    for block in got.values():
        total = total + block.astype(f32)
    total = total.astype(bf16)
    total = lax.psum_scatter(
        total, "dp", scatter_dimension=0, axis_index_groups=outer_groups(), tiled=True
    )
    return total[0]


def across(own):
    return {m: from_ctx(own, m) for m in range(2, lax.axis_size("ctx"), 2)}


def beside(blocks):
    out = {}
    for m, block in blocks.items():
        out[m] = block
        out[m + 1] = from_ctx(block, 1)
    return out


def place_ctx(blocks, dim=0):
    shape = blocks[0].shape
    place = lax.axis_index("ctx")
    full = jnp.zeros(shape[:dim] + (lax.axis_size("ctx"),) + shape[dim:], blocks[0].dtype)
    for m, block in blocks.items():
        full = lax.dynamic_update_index_in_dim(full, block, place ^ m, dim)
    return full


def chip_sum(part, m):
    return part(m).astype(f32) + from_ctx(part(m + 1), 1).astype(f32)


def far_sums(part):
    return {m: chip_sum(part, m).astype(bf16) for m in range(2, lax.axis_size("ctx"), 2)}


def send_far(sums):
    return {m: from_ctx(block, m) for m, block in sums.items()}


def total_of(near, got):
    for block in got.values():
        near = near + block.astype(f32)
    return near


def scatter_ctx(part):
    got = send_far(far_sums(part))
    return total_of(chip_sum(part, 0), got)


def exchange_ctx(blocks):
    moved = [m for m in range(2, lax.axis_size("ctx"))] + [1]
    return {0: blocks[0], **{m: from_ctx(blocks[m], m) for m in moved}}


def by_distance(blocks):
    place = lax.axis_index("ctx")
    return [
        lax.dynamic_index_in_dim(blocks, place ^ m, 0, False) for m in range(lax.axis_size("ctx"))
    ]


def sum_ctx(x):
    m = 1
    while m < lax.axis_size("ctx"):
        x = x + from_ctx(x, m)
        m *= 2
    return x


def sum_dp(x):
    count = lax.axis_size("dp")
    m = 1
    while m < count:
        x = x + lax.ppermute(x, "dp", [(i ^ m, i) for i in range(count)])
        m *= 2
    return x


def split_cols(a, block):
    count = lax.axis_size("ctx")
    rows, n = a.shape
    a = a.reshape(rows, n // (count * block), count, block)
    return a.transpose(2, 0, 1, 3).reshape(count, rows, n // count)


def join_cols(a, block):
    count, rows, n = a.shape
    a = a.reshape(count, rows, n // block, block)
    return a.transpose(1, 2, 0, 3).reshape(rows, count * n)


def own_cols(a, block):
    count = lax.axis_size("ctx")
    rows, n = a.shape
    a = a.reshape(rows, n // (count * block), count, block)
    a = lax.dynamic_index_in_dim(a, lax.axis_index("ctx"), 2, False)
    return a.reshape(rows, n // count)


def spread_cols(a, block):
    count = lax.axis_size("ctx")
    rows, n = a.shape
    a = a.reshape(rows, n // block, block)
    full = jnp.zeros((rows, n // block, count, block), a.dtype)
    full = lax.dynamic_update_index_in_dim(full, a, lax.axis_index("ctx"), 2)
    return full.reshape(rows, count * n)


def attention_window(total_len):
    reach = -(-(DOC_MOST - 1) // QBLOCK) * QBLOCK
    return min(reach, total_len - QBLOCK), min(reach + QBLOCK, total_len)


def attention_scores(total_len, q_ref, k_ref, col_ref, row_ref):
    back, window = attention_window(total_len)
    first = pl.program_id(1) * QBLOCK
    start = pl.multiple_of(jnp.maximum(first - back, 0), QBLOCK)
    keys = k_ref[pl.ds(start, window), :]
    scores = dot(q_ref[...], keys, NT) * HD ** (-0.5)
    query_place = first + lax.broadcasted_iota(jnp.int32, (QBLOCK, window), 0)
    key_place = start + lax.broadcasted_iota(jnp.int32, (QBLOCK, window), 1)
    key_seg = row_ref[0:1, pl.ds(start, window)]
    allowed = (key_place <= query_place) & (col_ref[:, 0:1] == key_seg)
    return start, window, keys, jnp.where(allowed, scores, -1e30)


def attend_kernel(total_len, q_ref, k_ref, v_ref, col_ref, row_ref, out_ref, log_ref):
    start, window, _, scores = attention_scores(total_len, q_ref, k_ref, col_ref, row_ref)
    peak = jnp.max(scores, axis=1, keepdims=True)
    expo = jnp.exp(scores - peak)
    log_total = peak + jnp.log(jnp.sum(expo, axis=1, keepdims=True))
    shares = jnp.exp(scores - log_total).astype(bf16)
    out_ref[...] = dot(shares, v_ref[pl.ds(start, window), :]).astype(out_ref.dtype)
    log_ref[...] = jnp.broadcast_to(log_total, log_ref.shape)


def attend_back_kernel(
    total_len, q_ref, k_ref, v_ref, col_ref, row_ref, log_ref, grad_ref, dq_ref, dk_ref, dv_ref
):
    @pl.when(pl.program_id(1) == 0)
    def _():
        dk_ref[...] = jnp.zeros_like(dk_ref)
        dv_ref[...] = jnp.zeros_like(dv_ref)

    start, window, keys, scores = attention_scores(total_len, q_ref, k_ref, col_ref, row_ref)
    shares = jnp.exp(scores - log_ref[:, 0:1])
    grad = grad_ref[...]
    grad_shares = dot(grad, v_ref[pl.ds(start, window), :], NT)
    inner = jnp.sum(shares * grad_shares, axis=1, keepdims=True)
    grad_scores = (shares * (grad_shares - inner)).astype(bf16)
    scale = HD ** (-0.5)
    dq_ref[...] = dot(grad_scores, keys) * scale
    span = pl.ds(start, window)
    dk_ref[span, :] += dot(grad_scores, q_ref[...], TN) * scale
    dv_ref[span, :] += dot(shares.astype(bf16), grad, TN)


def attention_specs(total_len, offset):
    tile = pl.BlockSpec((QBLOCK, HD), lambda h, i: (i, h))
    whole = pl.BlockSpec((total_len, HD), lambda h, i: (0, h))
    later = pl.BlockSpec((total_len, HD), lambda h, i: (0, h + offset))
    col = pl.BlockSpec((QBLOCK, 128), lambda h, i: (i, 0))
    row = pl.BlockSpec((8, total_len), lambda h, i: (0, 0))
    return tile, whole, later, col, row


def attention_call(queries, pairs, offset, seg_col, seg_row):
    total_len, width = queries.shape
    tile, whole, later, col, row = attention_specs(total_len, offset)
    return pl.pallas_call(
        functools.partial(attend_kernel, total_len),
        grid=(width // HD, total_len // QBLOCK),
        in_specs=[tile, whole, later, col, row],
        out_specs=[tile, tile],
        out_shape=[
            jax.ShapeDtypeStruct((total_len, width), bf16),
            jax.ShapeDtypeStruct((total_len, width), f32),
        ],
        compiler_params=pltpu.CompilerParams(vmem_limit_bytes=48 * 2**20),
        cost_estimate=pl.CostEstimate(flops=1, bytes_accessed=1, transcendentals=0),
        name="attend",
    )(queries, pairs, pairs, seg_col, seg_row)


def attention_back_call(queries, pairs, offset, seg_col, seg_row, log_total, grad):
    total_len, width = queries.shape
    tile, whole, later, col, row = attention_specs(total_len, offset)
    return pl.pallas_call(
        functools.partial(attend_back_kernel, total_len),
        grid=(width // HD, total_len // QBLOCK),
        in_specs=[tile, whole, later, col, row, tile, tile],
        out_specs=[tile, whole, whole],
        out_shape=[jax.ShapeDtypeStruct((total_len, width), f32)] * 3,
        compiler_params=pltpu.CompilerParams(vmem_limit_bytes=48 * 2**20),
        cost_estimate=pl.CostEstimate(flops=1, bytes_accessed=1, transcendentals=0),
        name="attend_back",
    )(queries, pairs, pairs, seg_col, seg_row, log_total, grad)


def pair_of(col, offset, j, left):
    a = offset + 2 * j
    return jnp.where(left, col[:, a : a + 1], col[:, a + 1 : a + 2])


def state_decay(col, j, left_rows):
    last = col[CHUNK - 1 : CHUNK, :]
    a = 64 + 2 * j
    return jnp.where(left_rows, last[:, a : a + 1], last[:, a + 1 : a + 2])


def scan_kernel(pairs, x_ref, k_ref, r_ref, col_ref, row_ref, skip_ref, y_ref, s_ref, state):
    @pl.when(pl.program_id(0) == 0)
    def _():
        state[...] = jnp.zeros_like(state)

    writes = k_ref[...].astype(bf16)
    reads = r_ref[...].astype(bf16)
    col = col_ref[...]
    row = row_ref[...]
    entering = state[...].astype(bf16)
    s_ref[0] = entering
    products = dot(reads, writes, NT)
    later = lax.broadcasted_iota(jnp.int32, (CHUNK, CHUNK), 0)
    earlier = lax.broadcasted_iota(jnp.int32, (CHUNK, CHUNK), 1)
    mask = (later >= earlier) & (col[:, 127:128] == row[16:17, :])
    left = lax.broadcasted_iota(jnp.int32, (CHUNK, 128), 1) < HEAD_M
    left_rows = lax.broadcasted_iota(jnp.int32, (128, STATE), 0) < HEAD_M
    through = dot(reads, entering, NT)
    for j in range(pairs):
        lanes = slice(128 * j, 128 * j + 128)
        x = x_ref[:, lanes]
        scaled = x * pair_of(col, 32, j, left)
        scaled_low = scaled.astype(bf16)
        outs = []
        for h in (2 * j, 2 * j + 1):
            spread = col[:, h : h + 1] - row[h : h + 1, :]
            mixing = jnp.exp(jnp.where(mask, spread, -1e30)) * products
            outs.append(dot(mixing.astype(bf16), scaled_low))
        y_ref[:, lanes] = (
            jnp.where(left, outs[0], outs[1])
            + pair_of(col, 64, j, left) * through[:, lanes]
            + skip_ref[0:1, lanes] * x
        )
        to_end = (scaled * pair_of(col, 96, j, left)).astype(bf16)
        state[lanes, :] = state_decay(col, j, left_rows) * state[lanes, :] + dot(to_end, writes, TN)


def scan_back_kernel(
    pairs,
    x_ref,
    k_ref,
    r_ref,
    col_ref,
    row_ref,
    skip_ref,
    y_ref,
    s_ref,
    dy_ref,
    sum_ref,
    dx_ref,
    dk_ref,
    dr_ref,
    red_ref,
    tot_ref,
    adjoint,
    keep,
):
    @pl.when(pl.program_id(0) == 0)
    def _():
        adjoint[...] = jnp.zeros_like(adjoint)

    writes = k_ref[...].astype(bf16)
    reads = r_ref[...].astype(bf16)
    col = col_ref[...]
    row = row_ref[...]
    entering = s_ref[0]
    products = dot(writes, reads, NT)
    earlier = lax.broadcasted_iota(jnp.int32, (CHUNK, CHUNK), 0)
    later = lax.broadcasted_iota(jnp.int32, (CHUNK, CHUNK), 1)
    mask = (later >= earlier) & (col[:, 127:128] == row[16:17, :])
    left = lax.broadcasted_iota(jnp.int32, (CHUNK, 128), 1) < HEAD_M
    left_rows = lax.broadcasted_iota(jnp.int32, (128, STATE), 0) < HEAD_M
    incoming = adjoint[...]
    incoming_low = incoming.astype(bf16)
    values = dot(writes, incoming_low, NT)
    grad_products = jnp.zeros((CHUNK, CHUNK), f32)
    grad_writes = jnp.zeros((CHUNK, STATE), f32)
    grad_reads = jnp.zeros((CHUNK, STATE), f32)
    tot_ref[0] = jnp.zeros(tot_ref.shape[1:], f32)
    for j in range(pairs):
        lanes = slice(128 * j, 128 * j + 128)
        x = x_ref[:, lanes]
        step = pair_of(col, 32, j, left)
        scaled = x * step
        scaled_low = scaled.astype(bf16)
        dy = dy_ref[:, lanes]
        dy_low = dy.astype(bf16)
        grads = []
        for side, h in enumerate((2 * j, 2 * j + 1)):
            spread = row[h : h + 1, :] - col[:, h : h + 1]
            decay = jnp.exp(jnp.where(mask, spread, -1e30))
            half = left if side == 0 else jnp.logical_not(left)
            grad_mixing = dot(jnp.where(half, scaled_low, jnp.zeros_like(scaled_low)), dy_low, NT)
            grad_products += grad_mixing * decay
            grads.append(dot((decay * products).astype(bf16), dy_low))
        grad_scaled = jnp.where(left, grads[0], grads[1])
        decay_end = pair_of(col, 96, j, left)
        to_end = (scaled * decay_end).astype(bf16)
        passed = to_end.astype(f32) * values[:, lanes]
        skip = skip_ref[0:1, lanes]
        flow = (
            dy_low.astype(f32) * (y_ref[:, lanes] - skip * x)
            - scaled_low.astype(f32) * grad_scaled
            - passed
        )
        grad_scaled += decay_end * values[:, lanes]
        dx_ref[:, lanes] = (step * grad_scaled + skip * dy).astype(bf16)
        from_start = (pair_of(col, 64, j, left) * dy).astype(bf16)
        grad_reads += dot(from_start, entering[lanes, :])
        grad_writes += dot(to_end, incoming_low[lanes, :])
        pieces = (flow, x * grad_scaled)
        for n, piece in enumerate(pieces):
            high = piece.astype(bf16)
            keep[2 * n, :, lanes] = high
            keep[2 * n + 1, :, lanes] = (piece - high.astype(f32)).astype(bf16)
        tot_ref[0, 1:2, lanes] = jnp.sum(passed, axis=0, keepdims=True)
        tot_ref[0, 2:3, lanes] = jnp.sum(dy * x, axis=0, keepdims=True)
        product = incoming[lanes, :] * entering[lanes, :].astype(f32)
        high = product.astype(bf16)
        low = (product - high.astype(f32)).astype(bf16)
        ones = jnp.ones((8, STATE), bf16)
        tot_ref[0, 0:1, lanes] = (dot(ones, high, NT) + dot(ones, low, NT))[0:1, :]
        adjoint[lanes, :] = state_decay(col, j, left_rows) * incoming[lanes, :] + dot(
            from_start, reads, TN
        )
    grad_products = grad_products.astype(bf16)
    dk_ref[...] = (grad_writes + dot(grad_products, reads)).astype(bf16)
    dr_ref[...] = (grad_reads + dot(grad_products, writes, TN)).astype(bf16)
    sums = sum_ref[...]
    red_ref[...] = (
        dot(keep[0], sums[0]) + dot(keep[1], sums[0]) + dot(keep[2], sums[1]) + dot(keep[3], sums[1])
    )


def scan_call(own, shared, col, row, skip, width):
    total_len = own.shape[0]
    count = total_len // CHUNK
    return pl.pallas_call(
        functools.partial(scan_kernel, width // 128),
        grid=(count,),
        in_specs=[
            pl.BlockSpec((CHUNK, width), lambda i: (i, 0)),
            pl.BlockSpec((CHUNK, STATE), lambda i: (i, 0)),
            pl.BlockSpec((CHUNK, STATE), lambda i: (i, 1)),
            pl.BlockSpec((CHUNK, 128), lambda i: (i, 0)),
            pl.BlockSpec((24, CHUNK), lambda i: (0, i)),
            pl.BlockSpec((8, width), lambda i: (0, 0)),
        ],
        out_specs=[
            pl.BlockSpec((CHUNK, width), lambda i: (i, 0)),
            pl.BlockSpec((1, width, STATE), lambda i: (i, 0, 0)),
        ],
        out_shape=[
            jax.ShapeDtypeStruct((total_len, width), f32),
            jax.ShapeDtypeStruct((count, width, STATE), bf16),
        ],
        scratch_shapes=[pltpu.VMEM((width, STATE), f32)],
        compiler_params=pltpu.CompilerParams(vmem_limit_bytes=48 * 2**20),
        cost_estimate=pl.CostEstimate(flops=1, bytes_accessed=1, transcendentals=0),
        name="state_scan",
    )(own, shared, shared, col, row, skip)


def scan_back_call(own, shared, col, row, skip, scanned, states, grad, width):
    total_len = own.shape[0]
    count = total_len // CHUNK
    owner = jnp.arange(width)[:, None] // HEAD_M
    lane = jnp.arange(128)[None, :]
    sums = jnp.stack([owner == lane, owner + 32 == lane]).astype(bf16)

    def back(i):
        return count - 1 - i

    return pl.pallas_call(
        functools.partial(scan_back_kernel, width // 128),
        grid=(count,),
        in_specs=[
            pl.BlockSpec((CHUNK, width), lambda i: (back(i), 0)),
            pl.BlockSpec((CHUNK, STATE), lambda i: (back(i), 0)),
            pl.BlockSpec((CHUNK, STATE), lambda i: (back(i), 1)),
            pl.BlockSpec((CHUNK, 128), lambda i: (back(i), 0)),
            pl.BlockSpec((24, CHUNK), lambda i: (0, back(i))),
            pl.BlockSpec((8, width), lambda i: (0, 0)),
            pl.BlockSpec((CHUNK, width), lambda i: (back(i), 0)),
            pl.BlockSpec((1, width, STATE), lambda i: (back(i), 0, 0)),
            pl.BlockSpec((CHUNK, width), lambda i: (back(i), 0)),
            pl.BlockSpec((2, width, 128), lambda i: (0, 0, 0)),
        ],
        out_specs=[
            pl.BlockSpec((CHUNK, width), lambda i: (back(i), 0)),
            pl.BlockSpec((CHUNK, STATE), lambda i: (back(i), 0)),
            pl.BlockSpec((CHUNK, STATE), lambda i: (back(i), 0)),
            pl.BlockSpec((CHUNK, 128), lambda i: (back(i), 0)),
            pl.BlockSpec((1, 8, width), lambda i: (back(i), 0, 0)),
        ],
        out_shape=[
            jax.ShapeDtypeStruct((total_len, width), bf16),
            jax.ShapeDtypeStruct((total_len, STATE), bf16),
            jax.ShapeDtypeStruct((total_len, STATE), bf16),
            jax.ShapeDtypeStruct((total_len, 128), f32),
            jax.ShapeDtypeStruct((count, 8, width), f32),
        ],
        scratch_shapes=[pltpu.VMEM((width, STATE), f32), pltpu.VMEM((4, CHUNK, width), bf16)],
        compiler_params=pltpu.CompilerParams(vmem_limit_bytes=48 * 2**20),
        cost_estimate=pl.CostEstimate(flops=1, bytes_accessed=1, transcendentals=0),
        name="state_scan_back",
    )(own, shared, shared, col, row, skip, scanned, states, grad, sums)


def feed_kernel(per_block, *refs):
    own_ref, side_ref, cot_ref, gate_ref, up_ref, down_ref = refs[:6]
    back_ref, mid_ref, hidden_ref, grad_gate_ref, grad_up_ref = refs[-5:]
    first = pl.program_id(0) < per_block
    mid = jnp.where(first, own_ref[...], side_ref[...])
    mid_ref[...] = mid
    gate = dot(mid, gate_ref[...])
    upper = dot(mid, up_ref[...])
    grad_hidden = dot(cot_ref[...], down_ref[...], NT)
    sigma = jax.nn.sigmoid(gate)
    gate_half = gate * sigma
    hidden_ref[...] = (gate_half * upper).astype(bf16)
    grad_gate = (grad_hidden * upper * (sigma * (1.0 + gate * (1.0 - sigma)))).astype(bf16)
    grad_up = (grad_hidden * gate_half).astype(bf16)
    grad_gate_ref[...] = grad_gate
    grad_up_ref[...] = grad_up
    back_ref[...] = (dot(grad_gate, gate_ref[...], NT) + dot(grad_up, up_ref[...], NT)).astype(bf16)


def feed_call(e, own, side, cot, w_gate, w_up, w_down, kept):
    length = own.shape[0]
    total_len = cot.shape[0]
    columns = w_gate.shape[1]
    tile = min(256, length)
    per_block = length // tile
    tiles = 2 * per_block

    def held(shape):
        return pl.BlockSpec(shape, lambda i: (0, 0), pipeline_mode=pl.Buffered(1))

    def spread(n):
        return pl.BlockSpec((tile, n), lambda i: (i + e * tiles, 0))

    kept_shapes = [(total_len, D)] + [(total_len, columns)] * 3
    return pl.pallas_call(
        functools.partial(feed_kernel, per_block),
        grid=(tiles,),
        in_specs=[
            pl.BlockSpec((tile, D), lambda i: (jnp.minimum(i, per_block - 1), 0)),
            pl.BlockSpec((tile, D), lambda i: (jnp.maximum(i - per_block, 0), 0)),
            spread(D),
            held(w_gate.shape),
            held(w_up.shape),
            held(w_down.shape),
        ]
        + [pl.BlockSpec(memory_space=pl.ANY)] * len(kept),
        out_specs=[
            pl.BlockSpec((tile, D), lambda i: (i, 0)),
            spread(D),
            spread(columns),
            spread(columns),
            spread(columns),
        ],
        out_shape=[jax.ShapeDtypeStruct((2 * length, D), bf16)]
        + [jax.ShapeDtypeStruct(shape, bf16) for shape in kept_shapes],
        input_output_aliases={6 + n: 1 + n for n in range(len(kept))},
        compiler_params=pltpu.CompilerParams(vmem_limit_bytes=56 * 2**20),
        cost_estimate=pl.CostEstimate(flops=1, bytes_accessed=1, transcendentals=0),
        name="feed_forward",
    )(own, side, cot, w_gate, w_up, w_down, *kept)


def token_sum_kernel(a_ref, b_ref, out_ref):
    out_ref[...] = dot(a_ref[...], b_ref[...], TN).astype(bf16)


def token_sum(a, b):
    total_len, rows = a.shape
    columns = b.shape[1]
    tile = math.gcd(rows, 512)
    return pl.pallas_call(
        token_sum_kernel,
        grid=(rows // tile,),
        in_specs=[
            pl.BlockSpec((total_len, tile), lambda i: (0, i)),
            pl.BlockSpec((total_len, columns), lambda i: (0, 0), pipeline_mode=pl.Buffered(1)),
        ],
        out_specs=pl.BlockSpec((tile, columns), lambda i: (i, 0)),
        out_shape=jax.ShapeDtypeStruct((rows, columns), bf16),
        compiler_params=pltpu.CompilerParams(vmem_limit_bytes=56 * 2**20),
        cost_estimate=pl.CostEstimate(flops=1, bytes_accessed=1, transcendentals=0),
        name="token_sum",
    )(a, b)


def normed_kernel(width, chip_ref, streams_ref, qz_ref, shared_ref, sq_w_ref, z_w_ref, sh_w_ref, out_ref):
    query = qz_ref.shape[1] - width
    total = dot(streams_ref[...], sq_w_ref[:, :width], NT)
    total += dot(qz_ref[:, :query], sq_w_ref[:, width:], NT)
    total += dot(qz_ref[:, query:], z_w_ref[...], NT)
    total += dot(shared_ref[...], sh_w_ref[...], NT)
    out_ref[...] = total.astype(bf16)


def normed_call(chip, rows, streams, qz, shared, w_sq, w_z, w_shared):
    width = streams.shape[1]
    tile = 256
    tiles = rows // tile

    def picked(n):
        return pl.BlockSpec((tile, n), lambda i, chip: (chip[0] * tiles + i, 0))

    def held(shape):
        return pl.BlockSpec(shape, lambda i, chip: (0, 0), pipeline_mode=pl.Buffered(1))

    return pl.pallas_call(
        functools.partial(normed_kernel, width),
        grid_spec=pltpu.PrefetchScalarGridSpec(
            num_scalar_prefetch=1,
            grid=(tiles,),
            in_specs=[
                picked(width),
                picked(qz.shape[1]),
                picked(shared.shape[1]),
                held(w_sq.shape),
                held(w_z.shape),
                held(w_shared.shape),
            ],
            out_specs=pl.BlockSpec((tile, D), lambda i, chip: (i, 0)),
        ),
        out_shape=jax.ShapeDtypeStruct((rows, D), bf16),
        compiler_params=pltpu.CompilerParams(vmem_limit_bytes=48 * 2**20),
        cost_estimate=pl.CostEstimate(flops=1, bytes_accessed=1, transcendentals=0),
        name="grad_normed",
    )(chip, streams, qz, shared, w_sq, w_z, w_shared)


def pack_in_kernel(count, place_ref, w_ref, own_ref, shared_ref):
    place = place_ref[0]
    width = DSSM // count
    first_z = width + QH * HD // count
    query = 2 * DSSM + 2 * STATE + HEADS_M
    for c in range(count):
        m = c ^ place
        for n in range(DSSM // (count * HD)):
            at = (n * count + c) * HD
            to = slice(n * HD, (n + 1) * HD)
            own_ref[m, :, to] = w_ref[:, DSSM + at : DSSM + at + HD].astype(bf16)
            to = slice(first_z + n * HD, first_z + (n + 1) * HD)
            own_ref[m, :, to] = w_ref[:, at : at + HD].astype(bf16)
        for n in range(QH // count):
            at = query + (n * count + c) * HD
            to = slice(width + n * HD, width + (n + 1) * HD)
            own_ref[m, :, to] = w_ref[:, at : at + HD].astype(bf16)
    shared_ref[:, : 2 * STATE] = w_ref[:, 2 * DSSM : 2 * DSSM + 2 * STATE].astype(bf16)
    shared_ref[:, 2 * STATE : SHARED - 128] = w_ref[:, query + QH * HD :].astype(bf16)
    steps = w_ref[:, query - HEADS_M : query - HEADS_M + 128]
    lane = lax.broadcasted_iota(jnp.int32, steps.shape, 1)
    shared_ref[:, SHARED - 128 :] = jnp.where(lane < HEADS_M, steps, 0.0).astype(bf16)


def pack_in(place, weight):
    rows = weight.shape[0]
    count = lax.axis_size("ctx")
    own_width = (2 * DSSM + QH * HD) // count
    return pl.pallas_call(
        functools.partial(pack_in_kernel, count),
        in_specs=[pl.BlockSpec(memory_space=pltpu.SMEM), pl.BlockSpec(memory_space=pltpu.VMEM)],
        out_specs=[pl.BlockSpec(memory_space=pltpu.VMEM)] * 2,
        out_shape=[
            jax.ShapeDtypeStruct((count, rows, own_width), bf16),
            jax.ShapeDtypeStruct((rows, SHARED), bf16),
        ],
        compiler_params=pltpu.CompilerParams(vmem_limit_bytes=48 * 2**20),
        name="pack_in",
    )(place, weight)


def pack_gate_up_kernel(count, place_ref, w_ref, out_ref):
    place = place_ref[0]
    blocks = FF // (count * HD)
    for c in range(count):
        m = c ^ place
        for n in range(2 * blocks):
            at = (n * count + c) * HD
            out_ref[m, :, n * HD : (n + 1) * HD] = w_ref[:, at : at + HD].astype(bf16)


def pack_gate_up(place, weight):
    rows = weight.shape[0]
    count = lax.axis_size("ctx")
    return pl.pallas_call(
        functools.partial(pack_gate_up_kernel, count),
        in_specs=[pl.BlockSpec(memory_space=pltpu.SMEM), pl.BlockSpec(memory_space=pltpu.VMEM)],
        out_specs=pl.BlockSpec(memory_space=pltpu.VMEM),
        out_shape=jax.ShapeDtypeStruct((count, rows, 2 * FF // count), bf16),
        compiler_params=pltpu.CompilerParams(vmem_limit_bytes=48 * 2**20),
        name="pack_gate_up",
    )(place, weight)


def update_kernel(count, spans, rate, place_ref, g_ref, *refs):
    tail_ref = refs[0] if len(refs) == 7 else None
    w_ref, first_ref, second_ref, new_w_ref, new_first_ref, new_second_ref = refs[-6:]
    place = place_ref[0]

    def update(cols, grad):
        new = adam_step(w_ref[:, cols], grad, first_ref[:, cols], second_ref[:, cols], rate)
        new_w_ref[:, cols], new_first_ref[:, cols], new_second_ref[:, cols] = new

    for first, columns, at in spans:
        for n in range(columns // (count * HD)):
            for c in range(count):
                start = first + (n * count + c) * HD
                grad = g_ref[c ^ place, :, at : at + HD].astype(f32)
                update(slice(start, start + HD), grad)
            at += HD
    if tail_ref is not None:
        update(slice(2 * DSSM, w_ref.shape[1]), tail_ref[...])


def update_dealt(place, got, tail, weight, first, second, spans, rate):
    rows, columns = weight.shape
    count = lax.axis_size("ctx")
    got = jnp.stack([got[m] for m in range(count)])
    block = 16

    def flat(n):
        return pl.BlockSpec((block, n), lambda i: (i, 0))

    tails = [] if tail is None else [tail]
    return pl.pallas_call(
        functools.partial(update_kernel, count, spans, rate),
        grid=(rows // block,),
        in_specs=[
            pl.BlockSpec(memory_space=pltpu.SMEM),
            pl.BlockSpec((count, block, got.shape[2]), lambda i: (0, i, 0)),
        ]
        + [flat(t.shape[1]) for t in tails]
        + [flat(columns)] * 3,
        out_specs=[flat(columns)] * 3,
        out_shape=[jax.ShapeDtypeStruct((rows, columns), f32)] * 3,
        compiler_params=pltpu.CompilerParams(vmem_limit_bytes=48 * 2**20),
        cost_estimate=pl.CostEstimate(flops=1, bytes_accessed=1, transcendentals=0),
        name="update",
    )(place, got, *tails, weight, first, second)


def rms_scale(values):
    return lax.rsqrt(jnp.mean(values * values, axis=-1, keepdims=True) + norm_eps)


def norm_back(grad_unit, unit, scale):
    return scale * (grad_unit - unit * jnp.mean(grad_unit * unit, axis=-1, keepdims=True))


def silu_slope(values):
    sigma = jax.nn.sigmoid(values)
    return sigma * (1.0 + values * (1.0 - sigma))


def split_small(small):
    widths = [D, D, DSSM, HEADS_M, HEADS_M, HEADS_M]
    pieces = []
    start = 0
    for count in widths:
        pieces.append(small[start : start + count])
        start += count
    return pieces


def adam_step(weight, grad, first, second, rate):
    first = beta_one * first + (1.0 - beta_one) * grad
    second = beta_two * second + (1.0 - beta_two) * grad * grad
    fixed_first = first / (1.0 - beta_one**STEP)
    fixed_second = second / (1.0 - beta_two**STEP)
    weight = weight - rate * (
        fixed_first / (jnp.sqrt(fixed_second) + adam_eps) + weight_decay * weight
    )
    return (weight, first, second)


def pad_lanes(a, width):
    return jnp.pad(a, ((0, 0), (0, width - a.shape[1])))


def shards(
    block_input,
    segment_ids,
    cotangent,
    in_weight,
    out_weight,
    gate_up_weight,
    down_weight,
    in_first,
    out_first,
    gate_up_first,
    down_first,
    in_second,
    out_second,
    gate_up_second,
    down_second,
    small_params,
    small_first,
    small_second,
):
    peers = lax.axis_size("ctx")
    groups = lax.axis_size("dp")
    place = lax.axis_index("ctx")
    length = block_input.shape[0] * block_input.shape[1]
    total_len = length * peers
    row_block = out_weight.shape[0]
    in_rows = in_weight.shape[0]
    strided = row_block == HD
    width = DSSM // peers
    heads = HEADS_M // peers
    query_heads = QH // peers
    query_width = query_heads * HD
    own_width = 2 * width + query_width
    ff_width = FF // peers
    pair_block = 2 * HEAD_M if strided else width
    query_block = HD if strided else query_width
    head_block = 2 if strided else heads
    gain_in, gain_mid, gain_mix, step_bias, decay_log, skip = split_small(small_params)

    place_arg = place.astype(jnp.int32).reshape(1)
    base = 2 * DSSM + 2 * STATE + HEADS_M
    query_end = base + QH * HD
    if strided:
        own_low, shared_low = pack_in(place_arg, in_weight)
        gu_low = pack_gate_up(place_arg, gate_up_weight)
        own_low = [own_low[m] for m in range(peers)]
        gu_low = [gu_low[m] for m in range(peers)]
    else:
        in_low = in_weight.astype(bf16)
        shared_low = jnp.concatenate(
            [
                in_low[:, 2 * DSSM : 2 * DSSM + 2 * STATE],
                in_low[:, query_end:],
                in_low[:, 2 * DSSM + 2 * STATE : base],
                jnp.zeros((in_rows, 128 - HEADS_M), bf16),
            ],
            axis=1,
        )
        own_low = jnp.concatenate(
            [
                split_cols(in_low[:, DSSM : 2 * DSSM], pair_block),
                split_cols(in_low[:, base:query_end], query_block),
                split_cols(in_low[:, :DSSM], pair_block),
            ],
            axis=2,
        )
        own_low = by_distance(own_low)
        gu_low = gate_up_weight.astype(bf16)
        gu_low = jnp.concatenate(
            [split_cols(gu_low[:, :FF], row_block), split_cols(gu_low[:, FF:], row_block)], axis=2
        )
        gu_low = by_distance(gu_low)
    seg_own = segment_ids.reshape(length)
    segments = place_ctx(beside({0: seg_own, **across(seg_own)})).reshape(total_len)
    own_rows = place_ctx(exchange_ctx(own_low)).reshape(peers * in_rows, own_width)
    x_own = block_input.reshape(length, D)
    shared_along = gather_outer_permuted(shared_low)
    out_low = out_weight.astype(bf16)
    down_low = down_weight.astype(bf16)
    own_rows, x_own, shared_along, gu_low, down_low, segments = fence(
        own_rows, x_own, shared_along, gu_low, down_low, segments
    )

    sq_width = width + query_width
    sq_along = gather_outer(own_rows[:, :sq_width])
    z_along = gather_outer(own_rows[:, sq_width:])
    x_far = across(x_own)
    shared_rows = place_dp(shared_along, gather_inner(shared_along))
    shared_rows = shared_rows.reshape((groups,) + shared_low.shape)
    down_inner = gather_inner(down_low)
    cot_own = cotangent.reshape(length, D)
    own_bias = own_cols(step_bias[None, :], head_block)
    own_decay = jnp.exp(own_cols(decay_log[None, :], head_block))
    own_skip = jnp.repeat(own_cols(skip[None, :], head_block), HEAD_M, axis=1)
    own_skip = jnp.broadcast_to(own_skip, (8, width))
    own_gain_mix = own_cols(gain_mix[None, :], pair_block)
    chunks = total_len // CHUNK
    seg_chunks = segments.reshape(chunks, CHUNK)
    seg_last = seg_chunks[:, -1:]
    seg_before = jnp.concatenate([jnp.full((1, 1), -1, seg_last.dtype), seg_last[:-1]], axis=0)
    entering = (seg_chunks == seg_before).astype(f32)[:, :, None]
    leaving = jnp.where(seg_chunks == seg_last, 0.0, -1e30)[:, :, None]
    seg_float = segments.astype(f32)
    seg_col = jnp.broadcast_to(seg_float[:, None], (total_len, 128))
    seg_row = jnp.broadcast_to(seg_float[None, :], (8, total_len))
    (x_own, x_far, shared_rows, gu_low, cot_own, sq_along, out_low, down_low, down_inner) = fence(
        x_own, x_far, shared_rows, gu_low, cot_own, sq_along, out_low, down_low, down_inner
    )
    own_bias, own_decay, own_skip, own_gain_mix, entering, leaving, seg_col, seg_row, x_far = fence(
        own_bias, own_decay, own_skip, own_gain_mix, entering, leaving, seg_col, seg_row, x_far
    )

    shared_far = across(shared_rows)
    if strided:
        out_along = gather_outer(out_low)
    sq_others = gather_inner(sq_along)
    tokens = place_ctx(beside({0: x_own, **x_far})).reshape(total_len, D)
    scale_in = rms_scale(tokens.astype(f32))
    normed = (tokens.astype(f32) * scale_in * gain_in).astype(bf16)
    normed, shared_rows, shared_far, sq_along, sq_others, z_along, cot_own, gu_low = fence(
        normed, shared_rows, shared_far, sq_along, sq_others, z_along, cot_own, gu_low
    )

    z_others = gather_inner(z_along)
    w_shared = place_ctx(beside({0: shared_rows, **shared_far}), 1).reshape(D, SHARED)
    pairs = dot(normed, w_shared[:, 2 * STATE : SHARED - 128]).astype(bf16)
    writes_reads = dot(normed, w_shared[:, : 2 * STATE])
    raw_all = dot(normed, w_shared[:, SHARED - 128 :])
    if not strided:
        out_along = {}
    normed, pairs, writes_reads, raw_all, z_along, z_others, out_along, cot_own, gu_low = fence(
        normed, pairs, writes_reads, raw_all, z_along, z_others, out_along, cot_own, gu_low
    )

    gu_rows = place_ctx(exchange_ctx(gu_low)).reshape(peers * in_rows, 2 * ff_width)
    gate_along = gather_outer(gu_rows[:, :ff_width])
    up_along = gather_outer(gu_rows[:, ff_width:])
    out_others = gather_inner(out_along) if strided else {}
    cot_far = across(cot_own)
    w_sq = place_dp(sq_along, sq_others).reshape(D, sq_width)
    streams = dot(normed, w_sq[:, :width])
    queries = dot(normed, w_sq[:, width:]).astype(bf16)
    raw_step = own_cols(raw_all[:, :HEADS_M], head_block)
    offset = KVH
    if query_heads < KVH:
        offset = query_heads
        own_kv = (place * query_heads * KVH // QH) * HD
        pairs = jnp.concatenate(
            [
                lax.dynamic_slice_in_dim(pairs, own_kv, query_width, 1),
                lax.dynamic_slice_in_dim(pairs, KVH * HD + own_kv, query_width, 1),
            ],
            axis=1,
        )
    step = jax.nn.softplus(raw_step + own_bias)
    rates = (-own_decay * step).reshape(chunks, CHUNK, heads)
    order = jnp.arange(CHUNK)
    lower = (order[:, None] >= order[None, :]).astype(f32)
    running = jnp.einsum("ts,csh->cth", lower, rates, precision=lax.Precision.HIGHEST)
    from_start = jnp.exp(running) * entering
    to_end = jnp.exp(jnp.where(leaving == 0.0, running[:, -1:, :] - running, -1e30))
    running = running.reshape(total_len, heads)
    col = jnp.concatenate(
        [
            pad_lanes(running, 32),
            pad_lanes(step, 32),
            pad_lanes(from_start.reshape(total_len, heads), 32),
            pad_lanes(to_end.reshape(total_len, heads), 31),
            seg_col[:, :1],
        ],
        axis=1,
    )
    row = jnp.concatenate([jnp.pad(running.T, ((0, 16 - heads), (0, 0))), seg_row], axis=0)

    scanned, states = scan_call(streams, writes_reads, col, row, own_skip, width)
    normed, scanned, queries, out_along, out_others, gate_along, cot_own, cot_far = fence(
        normed, scanned, queries, out_along, out_others, gate_along, cot_own, cot_far
    )

    gate_others = gather_inner(gate_along)
    inner_place = lax.rem(lax.axis_index("dp"), groups // 4)
    down_pair = jnp.stack([down_low] * (groups // 4))
    for k, block in down_inner.items():
        at = lax.rem(inner_place + k, groups // 4)
        down_pair = lax.dynamic_update_index_in_dim(down_pair, block, at, 0)
    w_down = gather_outer(down_pair).reshape(ff_width, D)
    cot = jnp.concatenate(
        [block for _, block in sorted(beside({0: cot_own, **cot_far}).items())], axis=0
    )
    w_z = place_dp(z_along, z_others).reshape(D, width)
    gate_z = dot(normed, w_z)
    attended, log_total = attention_call(queries, pairs, offset, seg_col, seg_row)
    gate_act = jax.nn.silu(gate_z)
    gated = scanned * gate_act
    square = sum_ctx(jnp.sum(gated * gated, axis=-1))
    scale_mix = lax.rsqrt(square / DSSM + norm_eps)[:, None]
    unit_mix = gated * scale_mix
    joined = jnp.concatenate([(unit_mix * own_gain_mix).astype(bf16), attended], axis=1)
    joined, gate_along, gate_others, up_along = fence(joined, gate_along, gate_others, up_along)
    up_others = gather_inner(up_along)
    if strided:
        w_out = place_dp(out_along, out_others).reshape(sq_width, D)
    else:
        whole_out = lax.all_gather(out_low, ("dp", "ctx"), axis=0, tiled=True)
        w_out = jnp.concatenate(
            [
                lax.dynamic_slice_in_dim(whole_out, place * width, width, 0),
                lax.dynamic_slice_in_dim(whole_out, DSSM + place * query_width, query_width, 0),
            ],
            axis=0,
        )

    chips = list(range(peers // 2))
    parity = place % 2

    def chip_rows(full, e):
        start = ((place // 2) ^ e) * 2 * length
        return lax.dynamic_slice_in_dim(full, start, 2 * length, 0)

    def core_part(parts):
        return lambda m: lax.dynamic_index_in_dim(parts[m // 2], (m % 2) ^ parity, 0, False)

    def mixed_rows(e):
        return dot(chip_rows(joined, e), w_out).astype(bf16).reshape(2, length, D)

    sums = far_sums(core_part({e: mixed_rows(e) for e in chips[1:]}))
    sums, joined, gate_along, gate_others = fence(sums, joined, gate_along, gate_others)
    w_gate = place_dp(gate_along, gate_others).reshape(D, ff_width)
    got = send_far(sums)
    near = chip_sum(core_part({0: mixed_rows(0)}), 0)
    got, near, up_others, w_gate = fence(got, near, up_others, w_gate)

    middle = x_own.astype(f32) + total_of(near, got)
    scale_mid = rms_scale(middle)
    unit_mid = middle * scale_mid
    mid_own = (unit_mid * gain_mid).astype(bf16)
    w_up = place_dp(up_along, up_others).reshape(D, ff_width)
    def feed_forward(e, own, side, kept):
        back, *kept = feed_call(e, own, side, cot, w_gate, w_up, w_down, kept)
        return back.reshape(2, length, D), kept

    far = across(mid_own)
    near_back, kept = feed_forward(0, mid_own, from_ctx(mid_own, 1), [])
    far, near_back, kept = fence(far, near_back, kept)
    far = beside(far)
    far_back = {}
    for e in chips[1:]:
        far_back[e], kept = feed_forward(e, far[2 * e], far[2 * e + 1], kept)
    sums = far_sums(lambda m: far_back[m // 2][m % 2])
    sums, near_back, kept = fence(sums, near_back, kept)
    normed_mid, hidden, grad_gate, grad_up = kept
    got = send_far(sums)
    near = chip_sum(lambda m: near_back[m], 0)
    grad_gate = token_sum(normed_mid, grad_gate)
    grad_down = token_sum(hidden, cot)
    got, near, grad_gate, grad_down, normed_mid, grad_up = fence(
        got, near, grad_gate, grad_down, normed_mid, grad_up
    )

    gate_parts = scatter_inner(grad_gate.reshape(groups, -1, ff_width))
    sum_down = lax.psum_scatter(
        grad_down.reshape(4, groups // 4, row_block, D),
        "dp",
        scatter_dimension=0,
        axis_index_groups=outer_groups(),
        tiled=True,
    )
    grad_normed_mid = total_of(near, got)
    grad_middle = cot_own.astype(f32) + norm_back(grad_normed_mid * gain_mid, unit_mid, scale_mid)
    grad_middle_low = grad_middle.astype(bf16)
    grad_middle_low, hidden, normed_mid, grad_up = fence(
        grad_middle_low, hidden, normed_mid, grad_up
    )

    far = across(grad_middle_low)
    beside_own = beside({0: grad_middle_low})
    result_part = dot(hidden, w_down).astype(bf16).reshape(peers, length, D)
    grad_up = token_sum(normed_mid, grad_up)
    far, beside_own, result_part, gate_parts, grad_up = fence(
        far, beside_own, result_part, gate_parts, grad_up
    )

    grad_mixed = place_ctx({**beside_own, **beside(far)}).reshape(total_len, D)
    sum_gate = scatter_outer(*gate_parts)
    up_parts = scatter_inner(grad_up.reshape(groups, -1, ff_width))
    grad_gain_mid = jnp.sum(grad_normed_mid * unit_mid, axis=0)
    sums = far_sums(lambda m: result_part[m])
    result_near = chip_sum(lambda m: result_part[m], 0)
    grad_joined = dot(grad_mixed, w_out, NT)
    if strided:
        grad_out = token_sum(joined, grad_mixed)
        out_parts = scatter_inner(grad_out.reshape(groups, row_block, D))
    else:
        grad_out = dot(joined, grad_mixed, TN)
        out_parts = ()
        spread = jnp.zeros((DSSM + QH * HD, D), f32)
        spread = lax.dynamic_update_slice_in_dim(spread, grad_out[:width], place * width, 0)
        spread = lax.dynamic_update_slice_in_dim(
            spread, grad_out[width:], DSSM + place * query_width, 0
        )
        sum_out = lax.psum_scatter(spread, ("dp", "ctx"), scatter_dimension=0, tiled=True)
    grad_attended = grad_joined[:, width:].astype(bf16)
    grad_mix_part = grad_joined[:, :width]
    grad_unit = grad_mix_part * own_gain_mix
    inner = sum_ctx(jnp.sum(grad_unit * unit_mix, axis=-1))[:, None] / DSSM
    grad_queries, grad_keys, grad_values = attention_back_call(
        queries, pairs, offset, seg_col, seg_row, log_total, grad_attended
    )
    grad_queries, inner, up_parts, out_parts, sums = fence(
        grad_queries, inner, up_parts, out_parts, sums
    )

    result_got = send_far(sums)
    inner_count = groups // 4
    down_own = lax.dynamic_index_in_dim(sum_down[0], inner_place, 0, False)
    down_got = {
        k: from_dp(
            lax.dynamic_index_in_dim(
                sum_down[0], lax.rem(inner_place + k, inner_count), 0, False
            ),
            0,
            -k,
        )
        for k in range(1, inner_count)
    }
    sum_down = total_of(down_own.astype(f32), down_got)
    sum_up = scatter_outer(*up_parts)
    if strided:
        sum_out = scatter_outer(*out_parts).astype(f32)
    grad_gain_mix = jnp.sum(grad_mix_part * unit_mix, axis=0)
    grad_gated = scale_mix * (grad_unit - unit_mix * inner)
    grad_scan = grad_gated * gate_act
    grad_z = grad_gated * scanned * silu_slope(gate_z)
    grad_qz = jnp.concatenate([grad_queries.astype(bf16), grad_z.astype(bf16)], axis=1)
    grad_in_qz = token_sum(normed, grad_qz)
    grad_in_qz, grad_scan = fence(grad_in_qz, grad_scan)

    qz_parts = scatter_inner(grad_in_qz.reshape(groups, -1, sq_width))
    grad_streams, grad_writes, grad_reads, reduced, totals = scan_back_call(
        streams, writes_reads, col, row, own_skip, scanned, states, grad_scan, width
    )
    grad_streams, grad_writes, grad_reads, reduced, totals, qz_parts, result_got = fence(
        grad_streams, grad_writes, grad_reads, reduced, totals, qz_parts, result_got
    )

    grad_in_streams = token_sum(normed, grad_streams)
    sum_qz = scatter_outer(*qz_parts)
    totals = totals.reshape(chunks, 8, heads, HEAD_M).sum(axis=3)
    last = from_start[:, -1, :] * totals[:, 0, :] + totals[:, 1, :]
    flow = reduced[:, :heads].reshape(chunks, CHUNK, heads)
    grad_rate = jnp.einsum("ts,cth->csh", lower, flow, precision=lax.Precision.HIGHEST)
    grad_rate = (grad_rate + last[:, None, :]).reshape(total_len, heads)
    grad_step = reduced[:, 32 : 32 + heads] - own_decay * grad_rate
    grad_raw = grad_step * jax.nn.sigmoid(raw_step + own_bias)
    if query_heads < KVH:
        blank = jnp.zeros((total_len, KVH * HD), f32)
        grad_keys = lax.dynamic_update_slice_in_dim(blank, grad_keys, own_kv, 1)
        grad_values = lax.dynamic_update_slice_in_dim(blank, grad_values, own_kv, 1)
    grad_shared = jnp.concatenate(
        [
            grad_writes,
            grad_reads,
            grad_keys.astype(bf16),
            grad_values.astype(bf16),
            pad_lanes(spread_cols(grad_raw.astype(bf16), head_block), 128),
        ],
        axis=1,
    )
    grad_in_streams, grad_shared, normed, grad_raw, grad_rate, totals, sum_gate, sum_up = fence(
        grad_in_streams, grad_shared, normed, grad_raw, grad_rate, totals, sum_gate, sum_up
    )

    def normed_rows(e):
        chip = ((place // 2) ^ e).astype(jnp.int32).reshape(1)
        part = normed_call(
            chip, 2 * length, grad_streams, grad_qz, grad_shared, w_sq, w_z, w_shared
        )
        return part.reshape(2, length, D)

    streams_parts = scatter_inner(grad_in_streams.reshape(groups, -1, width))
    grad_in_shared = token_sum(normed, grad_shared)
    far_rows = {e: normed_rows(e) for e in chips[1:]}
    streams_parts, grad_in_shared, far_rows, sum_gate, sum_up, sum_out, sum_down, result_got = fence(
        streams_parts, grad_in_shared, far_rows, sum_gate, sum_up, sum_out, sum_down, result_got
    )

    sum_streams = scatter_outer(*streams_parts)
    shared_part = grad_in_shared.reshape(groups, peers, in_rows, SHARED)

    def shared_of(m):
        return lax.dynamic_index_in_dim(shared_part, place ^ m, 1, False)

    shared_sums = far_sums(shared_of)
    sums = far_sums(core_part(far_rows))
    shared_sums, sums, shared_part, grad_shared = fence(shared_sums, sums, shared_part, grad_shared)

    got_shared = send_far(shared_sums)
    shared_near = chip_sum(shared_of, 0)
    near_rows = normed_rows(0)
    got_shared, shared_near, near_rows, sums = fence(got_shared, shared_near, near_rows, sums)

    got = send_far(sums)
    sum_shared = total_of(shared_near, got_shared).astype(bf16)
    sum_shared = scatter_outer(*scatter_inner(sum_shared)).astype(f32)
    near = chip_sum(core_part({0: near_rows}), 0)
    grad_gain_in = 0.0
    for e, rows in {0: near_rows, **far_rows}.items():
        unit = chip_rows(tokens, e).astype(f32) * chip_rows(scale_in, e)
        grad_gain_in += jnp.sum(rows.reshape(2 * length, D).astype(f32) * unit, axis=0)
    got, near, grad_gain_in = fence(got, near, grad_gain_in)

    sum_own = jnp.concatenate([sum_streams, sum_qz], axis=1)
    got_own = exchange_ctx(by_distance(sum_own.reshape(peers, in_rows, own_width)))
    sum_gate_up = jnp.concatenate([sum_gate, sum_up], axis=1)
    gu_sums = by_distance(sum_gate_up.reshape(peers, in_rows, 2 * ff_width))
    got_gate_up = exchange_ctx(gu_sums)
    grad_bias = jnp.sum(grad_raw, axis=0)
    grad_decay = jnp.sum(grad_rate * rates.reshape(total_len, heads), axis=0)
    grad_skip = jnp.sum(totals[:, 2, :], axis=0)

    result = middle + total_of(result_near, result_got)
    block_output = result.astype(bf16).reshape(block_input.shape)
    grad_normed = total_of(near, got)
    x_float = x_own.astype(f32)
    own_scale = rms_scale(x_float)
    own_unit = x_float * own_scale
    input_grad = grad_middle + norm_back(grad_normed * gain_in, own_unit, own_scale)
    input_grad = input_grad.reshape(block_input.shape)
    small_grad = jnp.concatenate(
        [
            grad_gain_in,
            grad_gain_mid,
            spread_cols(grad_gain_mix[None, :], pair_block)[0],
            spread_cols(grad_bias[None, :], head_block)[0],
            spread_cols(grad_decay[None, :], head_block)[0],
            spread_cols(grad_skip[None, :], head_block)[0],
        ]
    )
    small_grad = sum_dp(sum_ctx(small_grad))
    in_rate = rate_scale / math.sqrt(D)
    gate_up_state = (gate_up_weight, gate_up_first, gate_up_second)
    if strided:
        new_gate_up = update_dealt(
            place_arg, got_gate_up, None, *gate_up_state, ((0, 2 * FF, 0),), in_rate
        )
    else:
        got = place_ctx(got_gate_up).astype(f32)
        sum_gate_up = jnp.concatenate(
            [
                join_cols(got[:, :, :ff_width], row_block),
                join_cols(got[:, :, ff_width:], row_block),
            ],
            axis=1,
        )
        new_gate_up = adam_step(gate_up_weight, sum_gate_up, *gate_up_state[1:], in_rate)
    new_out = adam_step(
        out_weight, sum_out, out_first, out_second, rate_scale / math.sqrt(DSSM + QH * HD)
    )
    new_down = adam_step(
        down_weight, sum_down, down_first, down_second, rate_scale / math.sqrt(FF)
    )
    got = got_own
    placed = place_ctx({m: block[:, width:sq_width] for m, block in got.items()}).astype(f32)
    tail = jnp.concatenate(
        [
            sum_shared[:, : 2 * STATE],
            sum_shared[:, SHARED - 128 : SHARED - 128 + HEADS_M],
            join_cols(placed, query_block),
            sum_shared[:, 2 * STATE : SHARED - 128],
        ],
        axis=1,
    )
    if strided:
        spans = ((0, DSSM, sq_width), (DSSM, DSSM, 0))
        new_in = update_dealt(
            place_arg, got, tail, in_weight, in_first, in_second, spans, in_rate
        )
    else:
        got = place_ctx(got).astype(f32)
        sum_in = jnp.concatenate(
            [
                join_cols(got[:, :, sq_width:], pair_block),
                join_cols(got[:, :, :width], pair_block),
                tail,
            ],
            axis=1,
        )
        new_in = adam_step(in_weight, sum_in, in_first, in_second, in_rate)
    new_small = adam_step(small_params, small_grad, small_first, small_second, small_rate)
    return (block_output, input_grad, *new_in, *new_out, *new_gate_up, *new_down, *new_small)


def solution(mesh):
    rows = P(("dp", "ctx"), None)
    tokens = P("dp", "ctx", None)
    return jax.shard_map(
        shards,
        mesh=mesh,
        in_specs=(tokens, P("dp", "ctx"), tokens) + (rows,) * 12 + (P(),) * 3,
        out_specs=(tokens, tokens) + (rows,) * 12 + (P(),) * 3,
        check_vma=False,
    )
```

profile of v0, /device:TPU:0, one launch (start us, length us, event | category | flops | bytes accessed | tf_op | source)
XLA Modules:
  0.0 1021.9 jit_solution(4744434007716446646)
XLA Ops:
  43.6 11.3 %collective-permute-done.10 = bf16[4,64,1152]{2,1,0:T(8,128)(2,1)S(1)} collective-permute-done((bf16[4,64,1152]{2,1,0:T(8,128)(2,1)S(1)}, bf16[4,64,1152]{2,1,0:T(8,128)(2,1)S(1)}, u32[]{:S(2)}, u32[]{:S(2)}) %collective-permute-start.10) | collective-permute-done | bytes 589856 | tf_op jit(solution)/shard_map/ppermute | solution.py:56
  55.0 10.4 %collective-permute-done.11 = bf16[128,2048]{1,0:T(8,128)(2,1)S(1)} collective-permute-done((bf16[128,2048]{1,0:T(8,128)(2,1)S(1)}, bf16[128,2048]{1,0:T(8,128)(2,1)S(1)}, u32[]{:S(2)}, u32[]{:S(2)}) %collective-permute-start.11) | collective-permute-done | bytes 524320 | tf_op jit(solution)/shard_map/ppermute | solution.py:56
  66.2 20.4 %collective-permute-done.9 = bf16[512,2048]{1,0:T(8,128)(2,1)} collective-permute-done((bf16[512,2048]{1,0:T(8,128)(2,1)}, bf16[512,2048]{1,0:T(8,128)(2,1)}, u32[]{:S(2)}, u32[]{:S(2)}) %collective-permute-start.9) | collective-permute-done | bytes 2097184 | tf_op jit(solution)/shard_map/ppermute | solution.py:46
  104.0 8.7 multiply_convert_fusion.a_ref
  112.7 9.7 all-gather.16.cloned.1.call-done
  122.4 14.3 %collective-permute-done.15 = bf16[4,256,1024]{2,1,0:T(8,128)(2,1)} collective-permute-done((bf16[4,256,1024]{2,1,0:T(8,128)(2,1)}, bf16[4,256,1024]{2,1,0:T(8,128)(2,1)}, u32[]{:S(2)}, u32[]{:S(2)}) %collective-permute-start.15) | collective-permute-done | bytes 2097184 | tf_op jit(solution)/shard_map/ppermute | solution.py:56
  188.7 11.9 %fusion.17.x_ref = f32[2048,768]{1,0:T(8,128)} fusion(bf16[2048,2048]{1,0:T(8,128)(2,1)} %multiply_convert_fusion.a_ref, bf16[2048,1024]{1,0:T(8,128)(2,1)} %bitcast.374), kind=kOutput, calls=%fused_computation.60 | convolution fusion | flops 6442450944 | bytes 17825792 | tf_op jit(solution)/shard_map/dot_general | solution.py:41
  205.2 24.5 %state_scan.1 = (f32[2048,768]{1,0:T(8,128)}, bf16[8,768,256]{2,1,0:T(8,128)(2,1)S(1)}) custom-call(f32[2048,768]{1,0:T(8,128)} %fusion.17.x_ref, f32[2048,512]{1,0:T(8,128)} %fusion.22.k_ref.r_ref, f32[2048,512]{1,0:T(8,128)} %fusion.22.k_ref.r_ref, f32[2048,128]{1,0:T(8,128)S(1)} %copy.182.col_ref, f32[24,2048]{1,0:T(8,128)S(1)} %select_maximum_fusion.row_ref, ...), custom_call_target="tpu_custom_call" | custom-call | flops 1 | bytes 1 | tf_op jit(solution)/shard_map/state_scan/pallas_call | solution.py:460
  240.1 13.8 %multiply_reduce_fusion.3 = (f32[2048]{0:T(1024)S(1)}, f32[2048,768]{1,0:T(8,128)S(1)}, f32[2048,768]{1,0:T(8,128)}) fusion(f32[2048,768]{1,0:T(8,128)} %get-tuple-element.244.y_ref, bf16[2048,2048]{1,0:T(8,128)(2,1)} %multiply_convert_fusion.a_ref, bf16[2048,768]{1,0:T(8,128)(2,1)} %bitcast.380), kind=kOutput, calls=%fused_computation.12 | convolution fusion | flops 6453458944 | bytes 30416896 | tf_op jit(solution)/shard_map/dot_general | solution.py:41
  263.9 19.6 %attend.1 = (bf16[2048,256]{1,0:T(8,128)(2,1)S(1)}, f32[2048,256]{1,0:T(8,128)S(1)}) custom-call(bf16[2048,256]{1,0:T(8,128)(2,1)S(1)} %convolution_convert_fusion.4.q_ref, bf16[2048,512]{1,0:T(8,128)(2,1)} %convolution_convert_fusion.3.k_ref.v_ref, bf16[2048,512]{1,0:T(8,128)(2,1)} %convolution_convert_fusion.3.k_ref.v_ref, f32[2048,128]{1,0:T(8,128)S(1)} %copy.186.col_ref, ...), custom_call_target="tpu_custom_call" | custom-call | flops 1 | bytes 1 | tf_op jit(solution)/shard_map/attend/pallas_call | solution.py:282
  287.9 16.0 %collective-permute-done.26 = bf16[4,256,1024]{2,1,0:T(8,128)(2,1)} collective-permute-done((bf16[4,256,1024]{2,1,0:T(8,128)(2,1)}, bf16[4,256,1024]{2,1,0:T(8,128)(2,1)}, u32[]{:S(2)}, u32[]{:S(2)}) %collective-permute-start.26) | collective-permute-done | bytes 2097184 | tf_op jit(solution)/shard_map/ppermute | solution.py:56
  343.9 36.5 %collective-permute-done.30 = bf16[4,256,1024]{2,1,0:T(8,128)(2,1)S(1)} collective-permute-done((bf16[4,256,1024]{2,1,0:T(8,128)(2,1)S(1)}, bf16[4,256,1024]{2,1,0:T(8,128)(2,1)S(1)}, u32[]{:S(2)}, u32[]{:S(2)}) %collective-permute-start.30) | collective-permute-done | bytes 2097184 | tf_op jit(solution)/shard_map/ppermute | solution.py:56
  400.7 30.3 %feed_forward.2 = (bf16[1024,2048]{1,0:T(8,128)(2,1)}, bf16[2048,2048]{1,0:T(8,128)(2,1)}, bf16[2048,1024]{1,0:T(8,128)(2,1)}, bf16[2048,1024]{1,0:T(8,128)(2,1)}, bf16[2048,1024]{1,0:T(8,128)(2,1)}) custom-call(bf16[512,2048]{1,0:T(8,128)(2,1)} %multiply_convert_fusion.3.refs_0_, bf16[512,2048]{1,0:T(8,128)(2,1)} %collective-permute-done.32.refs_1_, ...), custom_call_target="tpu_custom_call" | custom-call | flops 1 | bytes 1 | tf_op jit(solution)/shard_map/feed_forward/pallas_call | solution.py:566
  441.8 30.3 %feed_forward.3 = (bf16[1024,2048]{1,0:T(8,128)(2,1)}, bf16[2048,2048]{1,0:T(8,128)(2,1)}, bf16[2048,1024]{1,0:T(8,128)(2,1)}, bf16[2048,1024]{1,0:T(8,128)(2,1)}, bf16[2048,1024]{1,0:T(8,128)(2,1)}) custom-call(bf16[512,2048]{1,0:T(8,128)(2,1)} %collective-permute-done.31.refs_0_, ...), custom_call_target="tpu_custom_call", output_to_operand_aliasing={{1}: (6, {}), {2}: (7, {}), {3}: (8, {}), {4}: (9, {})} | custom-call | flops 1 | bytes 1 | tf_op jit(solution)/shard_map/feed_forward/pallas_call | solution.py:566
  482.7 14.7 %token_sum.8 = bf16[1024,2048]{1,0:T(8,128)(2,1)} custom-call(bf16[2048,1024]{1,0:T(8,128)(2,1)} %get-tuple-element.298.a_ref, bf16[2048,2048]{1,0:T(8,128)(2,1)} %constant_dynamic-update-slice_fusion.refs_2_.b_ref), custom_call_target="tpu_custom_call" | custom-call | flops 1 | bytes 1 | tf_op jit(solution)/shard_map/token_sum/pallas_call | solution.py:602
  497.3 13.3 %token_sum.7 = bf16[2048,1024]{1,0:T(8,128)(2,1)} custom-call(bf16[2048,2048]{1,0:T(8,128)(2,1)} %get-tuple-element.300.a_ref, bf16[2048,1024]{1,0:T(8,128)(2,1)} %get-tuple-element.290.b_ref), custom_call_target="tpu_custom_call" | custom-call | flops 1 | bytes 1 | tf_op jit(solution)/shard_map/token_sum/pallas_call | solution.py:602
  515.0 15.3 %collective-permute-done.37 = bf16[512,2048]{1,0:T(8,128)(2,1)} collective-permute-done((bf16[512,2048]{1,0:T(8,128)(2,1)}, bf16[512,2048]{1,0:T(8,128)(2,1)}, u32[]{:S(2)}, u32[]{:S(2)}) %collective-permute-start.37) | collective-permute-done | bytes 2097184 | tf_op jit(solution)/shard_map/ppermute | solution.py:46
  547.1 13.7 %token_sum.9 = bf16[2048,1024]{1,0:T(8,128)(2,1)} custom-call(bf16[2048,2048]{1,0:T(8,128)(2,1)} %get-tuple-element.300.a_ref, bf16[2048,1024]{1,0:T(8,128)(2,1)} %get-tuple-element.301.b_ref), custom_call_target="tpu_custom_call" | custom-call | flops 1 | bytes 1 | tf_op jit(solution)/shard_map/token_sum/pallas_call | solution.py:602
  560.8 10.6 %convolution_convert_fusion = bf16[2048,2048]{1,0:T(8,128)(2,1)S(1)} fusion(bf16[2048,1024]{1,0:T(8,128)(2,1)} %get-tuple-element.298.a_ref, bf16[1024,2048]{1,0:T(8,128)(2,1)S(1)} %bitcast.396), kind=kOutput, calls=%fused_computation.6 | convolution fusion | flops 8594128896 | bytes 16777216 | tf_op jit(solution)/shard_map/dot_general | solution.py:41
  571.4 19.6 %collective-permute-done.39 = bf16[512,2048]{1,0:T(8,128)(2,1)} collective-permute-done((bf16[512,2048]{1,0:T(8,128)(2,1)}, bf16[512,2048]{1,0:T(8,128)(2,1)}, u32[]{:S(2)}, u32[]{:S(2)}) %collective-permute-start.39) | collective-permute-done | bytes 2097184 | tf_op jit(solution)/shard_map/ppermute | solution.py:46
  622.6 14.8 %token_sum.10 = bf16[1024,2048]{1,0:T(8,128)(2,1)} custom-call(bf16[2048,1024]{1,0:T(8,128)(2,1)} %pad_maximum_fusion.1.a_ref, bf16[2048,2048]{1,0:T(8,128)(2,1)} %bitcast.97.b_ref), custom_call_target="tpu_custom_call" | custom-call | flops 1 | bytes 1 | tf_op jit(solution)/shard_map/token_sum/pallas_call | solution.py:602
  642.9 12.6 %fusion.90 = f32[2048,1024]{1,0:T(8,128)S(1)} fusion(bf16[2048,2048]{1,0:T(8,128)(2,1)} %bitcast.97.b_ref, bf16[1024,2048]{1,0:T(8,128)(2,1)} %bitcast.67), kind=kOutput, calls=%fused_computation.276 | convolution fusion | flops 8589934592 | bytes 20971520 | tf_op jit(solution)/shard_map/dot_general | solution.py:41
  665.1 28.5 %attend_back.1 = (f32[2048,256]{1,0:T(8,128)S(1)}, f32[2048,256]{1,0:T(8,128)}, f32[2048,256]{1,0:T(8,128)}) custom-call(bf16[2048,256]{1,0:T(8,128)(2,1)S(1)} %convolution_convert_fusion.4.q_ref, bf16[2048,512]{1,0:T(8,128)(2,1)} %convolution_convert_fusion.3.k_ref.v_ref, bf16[2048,512]{1,0:T(8,128)(2,1)} %convolution_convert_fusion.3.k_ref.v_ref, ...), custom_call_target="tpu_custom_call" | custom-call | flops 1 | bytes 1 | tf_op jit(solution)/shard_map/attend_back/pallas_call | solution.py:300
  700.8 12.7 %fusion.19 = (f32[2048,768]{1,0:T(8,128)}, bf16[2048,768]{1,0:T(8,128)(2,1)S(1)}) fusion(f32[2048]{0:T(1024)S(1)} %add_multiply_fusion.1, f32[2048,768]{1,0:T(8,128)} %copy-done.23, f32[2048,1024]{1,0:T(8,128)} %copy-done.33, f32[768]{0:T(1024)S(1)} %copy-done.78, f32[2048]{0:T(1024)S(1)} %copy-done.74, f32[2048,768]{1,0:T(8,128)} %get-tuple-element.442, ...), kind=kLoop, calls=%fused_computation.64 | loop fusion | flops 26738688 | bytes 34622464 | tf_op jit(solution)/shard_map/mul | solution.py:1139
  716.1 13.3 %token_sum.11 = bf16[2048,1024]{1,0:T(8,128)(2,1)} custom-call(bf16[2048,2048]{1,0:T(8,128)(2,1)} %multiply_convert_fusion.a_ref, bf16[2048,1024]{1,0:T(8,128)(2,1)} %pad_maximum_fusion.5.b_ref.qz_ref), custom_call_target="tpu_custom_call" | custom-call | flops 1 | bytes 1 | tf_op jit(solution)/shard_map/token_sum/pallas_call | solution.py:602
  739.8 33.1 %state_scan_back.1 = (bf16[2048,768]{1,0:T(8,128)(2,1)}, bf16[2048,256]{1,0:T(8,128)(2,1)S(1)}, bf16[2048,256]{1,0:T(8,128)(2,1)S(1)}, f32[2048,128]{1,0:T(8,128)S(1)}, f32[8,8,768]{2,1,0:T(8,128)S(1)}) custom-call(f32[2048,768]{1,0:T(8,128)} %fusion.17.x_ref, f32[2048,512]{1,0:T(8,128)} %fusion.22.k_ref.r_ref, f32[2048,512]{1,0:T(8,128)} %fusion.22.k_ref.r_ref, ...), custom_call_target="tpu_custom_call" | custom-call | flops 1 | bytes 1 | tf_op jit(solution)/shard_map/state_scan_back/pallas_call | solution.py:496
  783.1 11.0 %token_sum.12 = bf16[2048,768]{1,0:T(8,128)(2,1)} custom-call(bf16[2048,2048]{1,0:T(8,128)(2,1)} %multiply_convert_fusion.a_ref, bf16[2048,768]{1,0:T(8,128)(2,1)} %get-tuple-element.320.b_ref.streams_ref), custom_call_target="tpu_custom_call" | custom-call | flops 1 | bytes 1 | tf_op jit(solution)/shard_map/token_sum/pallas_call | solution.py:602
  822.9 20.0 %grad_normed.2 = bf16[1024,2048]{1,0:T(8,128)(2,1)} custom-call(s32[1]{0:T(128)} %bitcast.121.chip_ref, bf16[2048,768]{1,0:T(8,128)(2,1)S(1)} %copy-done, bf16[2048,1024]{1,0:T(8,128)(2,1)} %pad_maximum_fusion.5.b_ref.qz_ref, bf16[2048,1152]{1,0:T(8,128)(2,1)} %pad_dynamic-update-slice_fusion.b_ref.shared_ref, bf16[2048,1024]{1,0:T(8,128)(2,1)} %bitcast.376, ...), custom_call_target="tpu_custom_call" | custom-call | flops 1 | bytes 1 | tf_op jit(solution)/shard_map/grad_normed/pallas_call | solution.py:637
  842.9 15.8 %token_sum.13 = bf16[2048,1152]{1,0:T(8,128)(2,1)} custom-call(bf16[2048,2048]{1,0:T(8,128)(2,1)} %multiply_convert_fusion.a_ref, bf16[2048,1152]{1,0:T(8,128)(2,1)} %pad_dynamic-update-slice_fusion.b_ref.shared_ref), custom_call_target="tpu_custom_call" | custom-call | flops 1 | bytes 1 | tf_op jit(solution)/shard_map/token_sum/pallas_call | solution.py:602
  905.3 19.9 %grad_normed.3 = bf16[1024,2048]{1,0:T(8,128)(2,1)} custom-call(s32[1]{0:T(128)} %bitcast.135.chip_ref, bf16[2048,768]{1,0:T(8,128)(2,1)S(1)} %copy-done, bf16[2048,1024]{1,0:T(8,128)(2,1)} %pad_maximum_fusion.5.b_ref.qz_ref, bf16[2048,1152]{1,0:T(8,128)(2,1)} %pad_dynamic-update-slice_fusion.b_ref.shared_ref, bf16[2048,1024]{1,0:T(8,128)(2,1)} %bitcast.377, ...), custom_call_target="tpu_custom_call" | custom-call | flops 1 | bytes 1 | tf_op jit(solution)/shard_map/grad_normed/pallas_call | solution.py:637
  942.7 7.8 collective-permute-done.62
  957.3 26.6 %collective-permute-done.57 = bf16[512,2048]{1,0:T(8,128)(2,1)} collective-permute-done((bf16[512,2048]{1,0:T(8,128)(2,1)}, bf16[512,2048]{1,0:T(8,128)(2,1)}, u32[]{:S(2)}, u32[]{:S(2)}) %collective-permute-start.57) | collective-permute-done | bytes 2097184 | tf_op jit(solution)/shard_map/ppermute | solution.py:46
  (633 shorter events, 445.0 us)
Async XLA Ops:
  7.2 79.3 %all-gather.14.cloned.1.call-start = ((), (), s32[]{:S(2)}) async-start(), calls=%async_computation.15 | async-start | bytes 2621440 | tf_op jit(solution)/shard_map/all_gather | solution.py:70
  38.1 84.3 %all-gather.16.cloned.1.call-start = ((), (), s32[]{:S(2)}) async-start(), calls=%async_computation.16 | async-start | bytes 1966080 | tf_op jit(solution)/shard_map/all_gather | solution.py:70
  38.1 48.4 %collective-permute-start.9 = (bf16[512,2048]{1,0:T(8,128)(2,1)}, bf16[512,2048]{1,0:T(8,128)(2,1)}, u32[]{:S(2)}, u32[]{:S(2)}) collective-permute-start(bf16[512,2048]{1,0:T(8,128)(2,1)} %bitcast.8), channel_id=1, source_target_pairs={{2,0},{3,1},{0,2},{1,3},{6,4},{7,5},{4,6},{5,7},{10,8},{11,9},{8,1... | collective-permute-start | bytes 6291464 | tf_op jit(solution)/shard_map/ppermute | solution.py:46
  42.0 127.3 %all-gather.18.cloned.1.call-start = ((), (), s32[]{:S(2)}) async-start(), calls=%async_computation.17 | async-start | bytes 2621440 | tf_op jit(solution)/shard_map/all_gather | solution.py:70
  88.7 47.9 %collective-permute-start.15 = (bf16[4,256,1024]{2,1,0:T(8,128)(2,1)}, bf16[4,256,1024]{2,1,0:T(8,128)(2,1)}, u32[]{:S(2)}, u32[]{:S(2)}) collective-permute-start(bf16[4,256,1024]{2,1,0:T(8,128)(2,1)} %bitcast.419), channel_id=1, source_target_pairs={{4,0},{0,4},{12,8},{8,12},{20,16},{16,20},{28,24},{24,28},{5,1},{1... | collective-permute-start | bytes 6291464 | tf_op jit(solution)/shard_map/ppermute | solution.py:56
  90.8 149.3 %all-gather.20.cloned.1.call-start = ((), (), s32[]{:S(2)}) async-start(), calls=%async_computation.18 | async-start | bytes 2621440 | tf_op jit(solution)/shard_map/all_gather | solution.py:70
  176.5 63.5 %collective-permute-start.19 = (bf16[4,128,2048]{2,1,0:T(8,128)(2,1)}, bf16[4,128,2048]{2,1,0:T(8,128)(2,1)}, u32[]{:S(2)}, u32[]{:S(2)}) collective-permute-start(bf16[4,128,2048]{2,1,0:T(8,128)(2,1)} %bitcast.421), channel_id=1, source_target_pairs={{4,0},{0,4},{12,8},{8,12},{20,16},{16,20},{28,24},{24,28},{5,1},{1... | collective-permute-start | bytes 6291464 | tf_op jit(solution)/shard_map/ppermute | solution.py:56
  178.0 62.1 %collective-permute-start.23 = (bf16[512,2048]{1,0:T(8,128)(2,1)}, bf16[512,2048]{1,0:T(8,128)(2,1)}, u32[]{:S(2)}, u32[]{:S(2)}) collective-permute-start(bf16[512,2048]{1,0:T(8,128)(2,1)} %bitcast.398), channel_id=1, source_target_pairs={{2,0},{3,1},{0,2},{1,3},{6,4},{7,5},{4,6},{5,7},{10,8},{11,9},{8,1... | collective-permute-start | bytes 6291464 | tf_op jit(solution)/shard_map/ppermute | solution.py:46
  188.7 99.2 %all-gather.22.cloned.1.call-start = ((), (), s32[]{:S(2)}) async-start(), calls=%async_computation.19 | async-start | bytes 2621440 | tf_op jit(solution)/shard_map/all_gather | solution.py:70
  240.0 160.7 %all-gather.12.cloned.1.call-start = ((), (), s32[]{:S(2)}) async-start(), calls=%async_computation.7 | async-start | bytes 5242880 | tf_op jit(solution)/shard_map/all_gather | solution.py:70
  256.0 47.9 %collective-permute-start.26 = (bf16[4,256,1024]{2,1,0:T(8,128)(2,1)}, bf16[4,256,1024]{2,1,0:T(8,128)(2,1)}, u32[]{:S(2)}, u32[]{:S(2)}) collective-permute-start(bf16[4,256,1024]{2,1,0:T(8,128)(2,1)} %bitcast.60), channel_id=1, source_target_pairs={{4,0},{0,4},{12,8},{8,12},{20,16},{16,20},{28,24},{24,28},{5,1},{1... | collective-permute-start | bytes 6291464 | tf_op jit(solution)/shard_map/ppermute | solution.py:56
  319.1 455.4 %reduce-scatter.14.cloned.1.call-start = ((), (), s32[]{:S(2)}) async-start(), calls=%async_computation.11 | async-start | bytes 5242880 | tf_op jit(solution)/shard_map/reduce_scatter | solution.py:1068
  332.4 48.0 %collective-permute-start.30 = (bf16[4,256,1024]{2,1,0:T(8,128)(2,1)S(1)}, bf16[4,256,1024]{2,1,0:T(8,128)(2,1)S(1)}, u32[]{:S(2)}, u32[]{:S(2)}) collective-permute-start(bf16[4,256,1024]{2,1,0:T(8,128)(2,1)S(1)} %bitcast.423), channel_id=1, source_target_pairs={{4,0},{0,4},{12,8},{8,12},{20,16},{16,20},{28,24},{24,28},{5,1},{1... | collective-permute-start | bytes 6291464 | tf_op jit(solution)/shard_map/ppermute | solution.py:56
  333.9 47.8 %collective-permute-start.28 = (bf16[512,2048]{1,0:T(8,128)(2,1)S(1)}, bf16[512,2048]{1,0:T(8,128)(2,1)}, u32[]{:S(2)}, u32[]{:S(2)}) collective-permute-start(bf16[512,2048]{1,0:T(8,128)(2,1)S(1)} %fusion.16), channel_id=1, source_target_pairs={{2,0},{3,1},{0,2},{1,3},{6,4},{7,5},{4,6},{5,7},{10,8},{11,9},{8,1... | collective-permute-start | bytes 6291464 | tf_op jit(solution)/shard_map/ppermute | solution.py:46
  334.5 58.3 %collective-permute-start.33 = (bf16[512,2048]{1,0:T(8,128)(2,1)S(1)}, bf16[512,2048]{1,0:T(8,128)(2,1)S(1)}, u32[]{:S(2)}, u32[]{:S(2)}) collective-permute-start(bf16[512,2048]{1,0:T(8,128)(2,1)S(1)} %bitcast.399), channel_id=1, source_target_pairs={{1,0},{0,1},{3,2},{2,3},{5,4},{4,5},{7,6},{6,7},{9,8},{8,9},{11,10... | collective-permute-start | bytes 6291464 | tf_op jit(solution)/shard_map/ppermute | solution.py:46
  334.5 63.1 %collective-permute-start.34 = (bf16[512,2048]{1,0:T(8,128)(2,1)}, bf16[512,2048]{1,0:T(8,128)(2,1)S(1)}, u32[]{:S(2)}, u32[]{:S(2)}) collective-permute-start(bf16[512,2048]{1,0:T(8,128)(2,1)} %collective-permute-done.23), channel_id=1, source_target_pairs={{1,0},{0,1},{3,2},{2,3},{5,4},{4,5},{7,6},{6,7},{9,8},{8,9},{11,10... | collective-permute-start | bytes 6291464 | tf_op jit(solution)/shard_map/ppermute | solution.py:46
  387.8 48.4 %collective-permute-start.31 = (bf16[512,2048]{1,0:T(8,128)(2,1)}, bf16[512,2048]{1,0:T(8,128)(2,1)}, u32[]{:S(2)}, u32[]{:S(2)}) collective-permute-start(bf16[512,2048]{1,0:T(8,128)(2,1)} %multiply_convert_fusion.3.refs_0_), channel_id=1, source_target_pairs={{2,0},{3,1},{0,2},{1,3},{6,4},{7,5},{4,6},{5,7},{10,8},{11,9},{8,1... | collective-permute-start | bytes 6291464 | tf_op jit(solution)/shard_map/ppermute | solution.py:46
  482.1 48.2 %collective-permute-start.37 = (bf16[512,2048]{1,0:T(8,128)(2,1)}, bf16[512,2048]{1,0:T(8,128)(2,1)}, u32[]{:S(2)}, u32[]{:S(2)}) collective-permute-start(bf16[512,2048]{1,0:T(8,128)(2,1)} %add_convert_fusion.4), channel_id=1, source_target_pairs={{2,0},{3,1},{0,2},{1,3},{6,4},{7,5},{4,6},{5,7},{10,8},{11,9},{8,1... | collective-permute-start | bytes 6291464 | tf_op jit(solution)/shard_map/ppermute | solution.py:46
  530.3 283.1 %reduce-scatter.8.cloned.1.call-start = ((), (), s32[]{:S(2)}) async-start(), calls=%async_computation.8 | async-start | bytes 2621440 | tf_op jit(solution)/shard_map/reduce_scatter | solution.py:112
  546.2 48.4 %collective-permute-start.41 = (bf16[4,256,1024]{2,1,0:T(8,128)(2,1)}, bf16[4,256,1024]{2,1,0:T(8,128)(2,1)}, u32[]{:S(2)}, u32[]{:S(2)}) collective-permute-start(bf16[4,256,1024]{2,1,0:T(8,128)(2,1)} %get-tuple-element.404), channel_id=1, source_target_pairs={{4,0},{0,4},{12,8},{8,12},{20,16},{16,20},{28,24},{24,28},{5,1},{1... | collective-permute-start | bytes 6291464 | tf_op jit(solution)/shard_map/ppermute | solution.py:56
  597.2 63.3 %collective-permute-start.48 = (bf16[512,2048]{1,0:T(8,128)(2,1)}, bf16[512,2048]{1,0:T(8,128)(2,1)}, u32[]{:S(2)}, u32[]{:S(2)}) collective-permute-start(bf16[512,2048]{1,0:T(8,128)(2,1)} %get-tuple-element.397), channel_id=1, source_target_pairs={{1,0},{0,1},{3,2},{2,3},{5,4},{4,5},{7,6},{6,7},{9,8},{8,9},{11,10... | collective-permute-start | bytes 6291464 | tf_op jit(solution)/shard_map/ppermute | solution.py:46
  600.7 94.2 %collective-permute-start.46 = (bf16[4,256,1024]{2,1,0:T(8,128)(2,1)}, bf16[4,256,1024]{2,1,0:T(8,128)(2,1)}, u32[]{:S(2)}, u32[]{:S(2)}) collective-permute-start(bf16[4,256,1024]{2,1,0:T(8,128)(2,1)} %get-tuple-element.402), channel_id=1, source_target_pairs={{4,0},{0,4},{12,8},{8,12},{20,16},{16,20},{28,24},{24,28},{5,1},{1... | collective-permute-start | bytes 6291464 | tf_op jit(solution)/shard_map/ppermute | solution.py:56
  605.5 208.0 %reduce-scatter.10.cloned.1.call-start = ((), (), s32[]{:S(2)}) async-start(), calls=%async_computation.9 | async-start | bytes 2621440 | tf_op jit(solution)/shard_map/reduce_scatter | solution.py:112
  641.7 53.3 %collective-permute-start.47 = (bf16[4,128,2048]{2,1,0:T(8,128)(2,1)S(1)}, bf16[4,128,2048]{2,1,0:T(8,128)(2,1)}, u32[]{:S(2)}, u32[]{:S(2)}) collective-permute-start(bf16[4,128,2048]{2,1,0:T(8,128)(2,1)S(1)} %get-tuple-element.400), channel_id=1, source_target_pairs={{4,0},{0,4},{12,8},{8,12},{20,16},{16,20},{28,24},{24,28},{5,1},{1... | collective-permute-start | bytes 6291464 | tf_op jit(solution)/shard_map/ppermute | solution.py:56
  699.1 161.7 %reduce-scatter.12.cloned.1.call-start = ((), (), s32[]{:S(2)}) async-start(), calls=%async_computation.10 | async-start | bytes 2621440 | tf_op jit(solution)/shard_map/reduce_scatter | solution.py:112
  734.3 48.8 %collective-permute-start.49 = (bf16[4,256,1024]{2,1,0:T(8,128)(2,1)}, bf16[4,256,1024]{2,1,0:T(8,128)(2,1)}, u32[]{:S(2)}, u32[]{:S(2)}) collective-permute-start(bf16[4,256,1024]{2,1,0:T(8,128)(2,1)} %get-tuple-element.398), channel_id=1, source_target_pairs={{4,0},{0,4},{12,8},{8,12},{20,16},{16,20},{28,24},{24,28},{5,1},{1... | collective-permute-start | bytes 6291464 | tf_op jit(solution)/shard_map/ppermute | solution.py:56
  734.4 48.7 %collective-permute-start.50 = (bf16[512,2048]{1,0:T(8,128)(2,1)}, bf16[512,2048]{1,0:T(8,128)(2,1)}, u32[]{:S(2)}, u32[]{:S(2)}) collective-permute-start(bf16[512,2048]{1,0:T(8,128)(2,1)} %fusion.12), channel_id=1, source_target_pairs={{2,0},{3,1},{0,2},{1,3},{6,4},{7,5},{4,6},{5,7},{10,8},{11,9},{8,1... | collective-permute-start | bytes 6291464 | tf_op jit(solution)/shard_map/ppermute | solution.py:46
  739.3 185.9 %reduce-scatter.18.cloned.1.call-start = ((), (), s32[]{:S(2)}) async-start(), calls=%async_computation.13 | async-start | bytes 2621440 | tf_op jit(solution)/shard_map/reduce_scatter | solution.py:112
  808.4 116.8 %reduce-scatter.16.cloned.1.call-start = ((), (), s32[]{:S(2)}) async-start(), calls=%async_computation.12 | async-start | bytes 1966080 | tf_op jit(solution)/shard_map/reduce_scatter | solution.py:112
  819.3 60.6 %collective-permute-start.42 = (bf16[512,2048]{1,0:T(8,128)(2,1)}, bf16[512,2048]{1,0:T(8,128)(2,1)}, u32[]{:S(2)}, u32[]{:S(2)}) collective-permute-start(bf16[512,2048]{1,0:T(8,128)(2,1)} %get-tuple-element.396), channel_id=1, source_target_pairs={{1,0},{0,1},{3,2},{2,3},{5,4},{4,5},{7,6},{6,7},{9,8},{8,9},{11,10... | collective-permute-start | bytes 6291464 | tf_op jit(solution)/shard_map/ppermute | solution.py:46
  875.3 108.7 %reduce-scatter.20.cloned.1.call-start = ((), (), s32[]{:S(2)}) async-start(), calls=%async_computation.14 | async-start | bytes 737280 | tf_op jit(solution)/shard_map/reduce_scatter | solution.py:112
  932.4 51.5 %collective-permute-start.57 = (bf16[512,2048]{1,0:T(8,128)(2,1)}, bf16[512,2048]{1,0:T(8,128)(2,1)}, u32[]{:S(2)}, u32[]{:S(2)}) collective-permute-start(bf16[512,2048]{1,0:T(8,128)(2,1)} %fusion.11), channel_id=1, source_target_pairs={{2,0},{3,1},{0,2},{1,3},{6,4},{7,5},{4,6},{5,7},{10,8},{11,9},{8,1... | collective-permute-start | bytes 6291464 | tf_op jit(solution)/shard_map/ppermute | solution.py:46
  (153 other events, 2341.3 us)
Sparse Core Ops, SparseCore 0:
  38.2 46.1 all-gather.13
  86.5 35.8 all-gather.15
  124.5 44.7 all-gather.17
  188.8 47.7 all-gather.19
  240.1 47.7 all-gather.21
  319.2 80.9 all-gather.11
  530.5 76.3 reduce-scatter.13
  609.2 44.3 reduce-scatter.7
  699.2 43.5 reduce-scatter.9
  745.6 43.1 reduce-scatter.11
  808.5 44.3 reduce-scatter.17
  875.4 37.2 reduce-scatter.15
  951.6 23.2 reduce-scatter.19
where the time goes:
time: 1030 us; the launch traced here: 1020 us
  Pallas kernels  314 us (30%)
  waiting for transfers between devices  242 us (23%)
  other arithmetic  161 us (16%)
  local copies, waits for them, and re-layouts  146 us (14%)
  matrix products  87 us (8%)
  starting transfers between devices  55.7 us (5%)
  between operations  16.1 us (2%)
    ppermute x51, waiting for transfers between devices, from_ctx(): return lax.ppermute(x, 'ctx', [(i ^ m, i) for i in range(count)])  114 us
    ppermute x17, waiting for transfers between devices, from_dp(): return lax.ppermute(x, 'dp', pairs)  111 us
    pallas_call x7, Pallas kernels, token_sum(): pl.pallas_call(token_sum_kernel, grid=(rows // tile,), in_specs=[pl.Block...  96.5 us
    dot_general x10, matrix products, dot(): return lax.dot_general(a, b, dims, preferred_element_type=f32)  85.7 us
    pallas_call x2, Pallas kernels, feed_call(): pl.pallas_call(functools.partial(feed_kernel, per_block), grid=(tiles,),...  60.6 us
    pallas_call x2, Pallas kernels, normed_call(): pl.pallas_call(functools.partial(normed_kernel, width), grid_spec=pltpu.P...  39.8 us
    pallas_call x1, Pallas kernels, scan_back_call(): pl.pallas_call(functools.partial(scan_back_kernel, width // 128), grid=(c...  33.1 us
    unnamed x216, local copies, waits for them, and re-layouts  29.6 us
  transfers between devices with their start and end apart: 84, of which 28 were waited for; matrix products, arithmetic and copies ran while one was open for 35% of the time, Pallas kernels for 28%

commit v1 on v0

--- a/solution.py
+++ b/solution.py
@@ -614,46 +614,74 @@
     )(a, b)
 
 
-def normed_kernel(width, chip_ref, streams_ref, qz_ref, shared_ref, sq_w_ref, z_w_ref, sh_w_ref, out_ref):
-    query = qz_ref.shape[1] - width
-    total = dot(streams_ref[...], sq_w_ref[:, :width], NT)
-    total += dot(qz_ref[:, :query], sq_w_ref[:, width:], NT)
-    total += dot(qz_ref[:, query:], z_w_ref[...], NT)
-    total += dot(shared_ref[...], sh_w_ref[...], NT)
+def normed_kernel(chip_ref, *refs):
+    grads, weights, out_ref = refs[:3], refs[3:6], refs[6]
+    total = dot(grads[0][...], weights[0][...], NT)
+    total += dot(grads[1][...], weights[1][...], NT)
+    total += dot(grads[2][...], weights[2][...], NT)
     out_ref[...] = total.astype(bf16)
 
 
-def normed_call(chip, rows, streams, qz, shared, w_sq, w_z, w_shared):
-    width = streams.shape[1]
+def normed_call(chip, rows, grads, weights):
     tile = 256
     tiles = rows // tile
 
-    def picked(n):
-        return pl.BlockSpec((tile, n), lambda i, chip: (chip[0] * tiles + i, 0))
-
-    def held(shape):
-        return pl.BlockSpec(shape, lambda i, chip: (0, 0), pipeline_mode=pl.Buffered(1))
+    def picked(grad):
+        return pl.BlockSpec((tile, grad.shape[1]), lambda i, chip: (chip[0] * tiles + i, 0))
+
+    def held(weight):
+        return pl.BlockSpec(weight.shape, lambda i, chip: (0, 0), pipeline_mode=pl.Buffered(1))
 
     return pl.pallas_call(
-        functools.partial(normed_kernel, width),
+        normed_kernel,
         grid_spec=pltpu.PrefetchScalarGridSpec(
             num_scalar_prefetch=1,
             grid=(tiles,),
-            in_specs=[
-                picked(width),
-                picked(qz.shape[1]),
-                picked(shared.shape[1]),
-                held(w_sq.shape),
-                held(w_z.shape),
-                held(w_shared.shape),
-            ],
+            in_specs=[picked(grad) for grad in grads] + [held(weight) for weight in weights],
             out_specs=pl.BlockSpec((tile, D), lambda i, chip: (i, 0)),
         ),
         out_shape=jax.ShapeDtypeStruct((rows, D), bf16),
         compiler_params=pltpu.CompilerParams(vmem_limit_bytes=48 * 2**20),
         cost_estimate=pl.CostEstimate(flops=1, bytes_accessed=1, transcendentals=0),
         name="grad_normed",
-    )(chip, streams, qz, shared, w_sq, w_z, w_shared)
+    )(chip, *grads, *weights)
+
+
+def place_rows_kernel(place_ref, *refs):
+    for m, block_ref in enumerate(refs[:-1]):
+
+        @pl.when(pl.program_id(0) == m)
+        def _():
+            refs[-1][...] = block_ref[...]
+
+
+def place_rows(place, blocks):
+    count = len(blocks)
+    rows, columns = blocks[0].shape
+    tile = min(256, rows)
+    tiles = rows // tile
+
+    def source(k):
+        def at(m, i, place):
+            return jnp.where(m == k, i, jnp.where(m < k, 0, tiles - 1)), 0
+
+        return pl.BlockSpec((tile, columns), at)
+
+    return pl.pallas_call(
+        place_rows_kernel,
+        grid_spec=pltpu.PrefetchScalarGridSpec(
+            num_scalar_prefetch=1,
+            grid=(count, tiles),
+            in_specs=[source(k) for k in range(count)],
+            out_specs=pl.BlockSpec(
+                (tile, columns), lambda m, i, place: ((place[0] ^ m) * tiles + i, 0)
+            ),
+        ),
+        out_shape=jax.ShapeDtypeStruct((count * rows, columns), blocks[0].dtype),
+        compiler_params=pltpu.CompilerParams(vmem_limit_bytes=48 * 2**20),
+        cost_estimate=pl.CostEstimate(flops=1, bytes_accessed=1, transcendentals=0),
+        name="place_rows",
+    )(place, *[blocks[m] for m in range(count)])
 
 
 def pack_in_kernel(count, place_ref, w_ref, own_ref, shared_ref):
@@ -877,20 +905,21 @@
             [split_cols(gu_low[:, :FF], row_block), split_cols(gu_low[:, FF:], row_block)], axis=2
         )
         gu_low = by_distance(gu_low)
-    seg_own = segment_ids.reshape(length)
-    segments = place_ctx(beside({0: seg_own, **across(seg_own)})).reshape(total_len)
     own_rows = place_ctx(exchange_ctx(own_low)).reshape(peers * in_rows, own_width)
     x_own = block_input.reshape(length, D)
+    seg_own = segment_ids.reshape(length)
+    own_rows, x_own, shared_low, gu_low, seg_own = fence(
+        own_rows, x_own, shared_low, gu_low, seg_own
+    )
+
+    sq_width = width + query_width
+    s_along = gather_outer(own_rows[:, :width])
+    qz_along = gather_outer(own_rows[:, width:])
+    seg_far = across(seg_own)
+    segments = place_ctx(beside({0: seg_own, **seg_far})).reshape(total_len)
     shared_along = gather_outer_permuted(shared_low)
     out_low = out_weight.astype(bf16)
     down_low = down_weight.astype(bf16)
-    own_rows, x_own, shared_along, gu_low, down_low, segments = fence(
-        own_rows, x_own, shared_along, gu_low, down_low, segments
-    )
-
-    sq_width = width + query_width
-    sq_along = gather_outer(own_rows[:, :sq_width])
-    z_along = gather_outer(own_rows[:, sq_width:])
     x_far = across(x_own)
     shared_rows = place_dp(shared_along, gather_inner(shared_along))
     shared_rows = shared_rows.reshape((groups,) + shared_low.shape)
@@ -910,8 +939,8 @@
     seg_float = segments.astype(f32)
     seg_col = jnp.broadcast_to(seg_float[:, None], (total_len, 128))
     seg_row = jnp.broadcast_to(seg_float[None, :], (8, total_len))
-    (x_own, x_far, shared_rows, gu_low, cot_own, sq_along, out_low, down_low, down_inner) = fence(
-        x_own, x_far, shared_rows, gu_low, cot_own, sq_along, out_low, down_low, down_inner
+    (x_own, x_far, shared_rows, gu_low, cot_own, s_along, out_low, down_low, down_inner) = fence(
+        x_own, x_far, shared_rows, gu_low, cot_own, s_along, out_low, down_low, down_inner
     )
     own_bias, own_decay, own_skip, own_gain_mix, entering, leaving, seg_col, seg_row, x_far = fence(
         own_bias, own_decay, own_skip, own_gain_mix, entering, leaving, seg_col, seg_row, x_far
@@ -920,33 +949,33 @@
     shared_far = across(shared_rows)
     if strided:
         out_along = gather_outer(out_low)
-    sq_others = gather_inner(sq_along)
-    tokens = place_ctx(beside({0: x_own, **x_far})).reshape(total_len, D)
+    s_others = gather_inner(s_along)
+    tokens = place_rows(place_arg, beside({0: x_own, **x_far}))
     scale_in = rms_scale(tokens.astype(f32))
     normed = (tokens.astype(f32) * scale_in * gain_in).astype(bf16)
-    normed, shared_rows, shared_far, sq_along, sq_others, z_along, cot_own, gu_low = fence(
-        normed, shared_rows, shared_far, sq_along, sq_others, z_along, cot_own, gu_low
-    )
-
-    z_others = gather_inner(z_along)
+    normed, shared_rows, shared_far, s_along, s_others, qz_along, cot_own, gu_low = fence(
+        normed, shared_rows, shared_far, s_along, s_others, qz_along, cot_own, gu_low
+    )
+
+    qz_others = gather_inner(qz_along)
     w_shared = place_ctx(beside({0: shared_rows, **shared_far}), 1).reshape(D, SHARED)
     pairs = dot(normed, w_shared[:, 2 * STATE : SHARED - 128]).astype(bf16)
     writes_reads = dot(normed, w_shared[:, : 2 * STATE])
     raw_all = dot(normed, w_shared[:, SHARED - 128 :])
     if not strided:
         out_along = {}
-    normed, pairs, writes_reads, raw_all, z_along, z_others, out_along, cot_own, gu_low = fence(
-        normed, pairs, writes_reads, raw_all, z_along, z_others, out_along, cot_own, gu_low
+    normed, pairs, writes_reads, raw_all, cot_own, gu_low = fence(
+        normed, pairs, writes_reads, raw_all, cot_own, gu_low
     )
 
     gu_rows = place_ctx(exchange_ctx(gu_low)).reshape(peers * in_rows, 2 * ff_width)
     gate_along = gather_outer(gu_rows[:, :ff_width])
     up_along = gather_outer(gu_rows[:, ff_width:])
+    cot_far = across(cot_own)
+    w_streams = place_dp(s_along, s_others).reshape(D, width)
+    streams = dot(normed, w_streams)
+    streams, out_along = fence(streams, out_along)
     out_others = gather_inner(out_along) if strided else {}
-    cot_far = across(cot_own)
-    w_sq = place_dp(sq_along, sq_others).reshape(D, sq_width)
-    streams = dot(normed, w_sq[:, :width])
-    queries = dot(normed, w_sq[:, width:]).astype(bf16)
     raw_step = own_cols(raw_all[:, :HEADS_M], head_block)
     offset = KVH
     if query_heads < KVH:
@@ -980,8 +1009,8 @@
     row = jnp.concatenate([jnp.pad(running.T, ((0, 16 - heads), (0, 0))), seg_row], axis=0)
 
     scanned, states = scan_call(streams, writes_reads, col, row, own_skip, width)
-    normed, scanned, queries, out_along, out_others, gate_along, cot_own, cot_far = fence(
-        normed, scanned, queries, out_along, out_others, gate_along, cot_own, cot_far
+    normed, scanned, qz_along, qz_others, out_along, out_others, gate_along, cot_own, cot_far = fence(
+        normed, scanned, qz_along, qz_others, out_along, out_others, gate_along, cot_own, cot_far
     )
 
     gate_others = gather_inner(gate_along)
@@ -994,8 +1023,9 @@
     cot = jnp.concatenate(
         [block for _, block in sorted(beside({0: cot_own, **cot_far}).items())], axis=0
     )
-    w_z = place_dp(z_along, z_others).reshape(D, width)
-    gate_z = dot(normed, w_z)
+    w_qz = place_dp(qz_along, qz_others).reshape(D, sq_width)
+    queries = dot(normed, w_qz[:, :query_width]).astype(bf16)
+    gate_z = dot(normed, w_qz[:, query_width:])
     attended, log_total = attention_call(queries, pairs, offset, seg_col, seg_row)
     gate_act = jax.nn.silu(gate_z)
     gated = scanned * gate_act
@@ -1004,7 +1034,6 @@
     unit_mix = gated * scale_mix
     joined = jnp.concatenate([(unit_mix * own_gain_mix).astype(bf16), attended], axis=1)
     joined, gate_along, gate_others, up_along = fence(joined, gate_along, gate_others, up_along)
-    up_others = gather_inner(up_along)
     if strided:
         w_out = place_dp(out_along, out_others).reshape(sq_width, D)
     else:
@@ -1031,7 +1060,10 @@
         return dot(chip_rows(joined, e), w_out).astype(bf16).reshape(2, length, D)
 
     sums = far_sums(core_part({e: mixed_rows(e) for e in chips[1:]}))
-    sums, joined, gate_along, gate_others = fence(sums, joined, gate_along, gate_others)
+    sums, joined, gate_along, gate_others, up_along = fence(
+        sums, joined, gate_along, gate_others, up_along
+    )
+    up_others = gather_inner(up_along)
     w_gate = place_dp(gate_along, gate_others).reshape(D, ff_width)
     got = send_far(sums)
     near = chip_sum(core_part({0: mixed_rows(0)}), 0)
@@ -1087,7 +1119,7 @@
         far, beside_own, result_part, gate_parts, grad_up
     )
 
-    grad_mixed = place_ctx({**beside_own, **beside(far)}).reshape(total_len, D)
+    grad_mixed = place_rows(place_arg, {**beside_own, **beside(far)})
     sum_gate = scatter_outer(*gate_parts)
     up_parts = scatter_inner(grad_up.reshape(groups, -1, ff_width))
     grad_gain_mid = jnp.sum(grad_normed_mid * unit_mid, axis=0)
@@ -1179,9 +1211,8 @@
 
     def normed_rows(e):
         chip = ((place // 2) ^ e).astype(jnp.int32).reshape(1)
-        part = normed_call(
-            chip, 2 * length, grad_streams, grad_qz, grad_shared, w_sq, w_z, w_shared
-        )
+        grads = grad_streams, grad_qz, grad_shared
+        part = normed_call(chip, 2 * length, grads, (w_streams, w_qz, w_shared))
         return part.reshape(2, length, D)
 
     streams_parts = scatter_inner(grad_in_streams.reshape(groups, -1, width))

time: 1030 us -> 1020 us (level)
  Pallas kernels: 314 us -> 335 us
  local copies, waits for them, and re-layouts: 146 us -> 126 us
    ppermute x17, waiting for transfers between devices: 111 us -> 63.3 us  [from_dp(): return lax.ppermute(x, 'dp', pairs)]
    ppermute x51, waiting for transfers between devices: 114 us -> 145 us  [from_ctx(): return lax.ppermute(x, 'ctx', [(i ^ m, i) for i in range(count)])]
    pallas_call x2 -> x4, Pallas kernels: 39.8 us -> 57.8 us  [the longest x2 39.6 us: normed_call(): pl.pallas_call(normed_kernel, grid_spec=pltpu.PrefetchScalarGridSpec(num_...]
    dynamic_update_slice x27 -> x19, local copies, waits for them, and re-layouts: 26.8 us -> 8.97 us  [place_ctx(): full = lax.dynamic_update_index_in_dim(full, block, place ^ m, dim)]
    unnamed x216 -> x232, local copies, waits for them, and re-layouts: 29.6 us -> 28.2 us
  transfers between devices with their start and end apart: 84 -> 84, of which waited for: 28 -> 33; matrix products, arithmetic and copies ran while one was open for 35% -> 33% of each run, Pallas kernels for 28% -> 30%
where the time goes in v1:
time: 1020 us; the launch traced here: 1010 us
  Pallas kernels  335 us (33%)
  waiting for transfers between devices  232 us (23%)
  other arithmetic  161 us (16%)
  local copies, waits for them, and re-layouts  126 us (12%)
  matrix products  85.7 us (8%)
  starting transfers between devices  55.7 us (5%)
  between operations  16 us (2%)
    ppermute x51, waiting for transfers between devices, from_ctx(): return lax.ppermute(x, 'ctx', [(i ^ m, i) for i in range(count)])  145 us
    pallas_call x7, Pallas kernels, token_sum(): pl.pallas_call(token_sum_kernel, grid=(rows // tile,), in_specs=[pl.Block...  97 us
    dot_general x10, matrix products, dot(): return lax.dot_general(a, b, dims, preferred_element_type=f32)  84.5 us
    ppermute x17, waiting for transfers between devices, from_dp(): return lax.ppermute(x, 'dp', pairs)  63.3 us
    pallas_call x2, Pallas kernels, feed_call(): pl.pallas_call(functools.partial(feed_kernel, per_block), grid=(tiles,),...  60.5 us
    pallas_call x2, Pallas kernels, normed_call(): pl.pallas_call(normed_kernel, grid_spec=pltpu.PrefetchScalarGridSpec(num_...  39.6 us
    pallas_call x1, Pallas kernels, scan_back_call(): pl.pallas_call(functools.partial(scan_back_kernel, width // 128), grid=(c...  34.1 us
    ppermute x51, starting transfers between devices, from_ctx(): return lax.ppermute(x, 'ctx', [(i ^ m, i) for i in range(count)])  29.9 us
  transfers between devices with their start and end apart: 84, of which 33 were waited for; matrix products, arithmetic and copies ran while one was open for 33% of the time, Pallas kernels for 30%

profile of v1, /device:TPU:0, one launch (start us, length us, event | category | flops | bytes accessed | tf_op | source)
XLA Modules:
  0.0 1011.1 jit_solution(14060238347256884779)
XLA Ops:
  50.8 13.4 %collective-permute-done.7 = bf16[4,64,1152]{2,1,0:T(8,128)(2,1)S(1)} collective-permute-done((bf16[4,64,1152]{2,1,0:T(8,128)(2,1)S(1)}, bf16[4,64,1152]{2,1,0:T(8,128)(2,1)S(1)}, u32[]{:S(2)}, u32[]{:S(2)}) %collective-permute-start.7) | collective-permute-done | bytes 589856 | tf_op jit(solution)/shard_map/ppermute | solution.py:56
  64.3 20.9 %collective-permute-done.3.refs_2_ = bf16[512,2048]{1,0:T(8,128)(2,1)} collective-permute-done((bf16[512,2048]{1,0:T(8,128)(2,1)S(1)}, bf16[512,2048]{1,0:T(8,128)(2,1)}, u32[]{:S(2)}, u32[]{:S(2)}) %collective-permute-start.3) | collective-permute-done | bytes 2097184 | tf_op jit(solution)/shard_map/ppermute | solution.py:46
  92.7 9.8 place_rows.2
  107.7 8.8 fusion.2.a_ref
  116.5 19.1 %all-gather.16.cloned.1.call-done = bf16[1024,1024]{1,0:T(8,128)(2,1)} async-done(((bf16[256,1024]{1,0:T(8,128)(2,1)}), bf16[1024,1024]{1,0:T(8,128)(2,1)}) %all-gather.16.cloned.1.call-update) | async-done | bytes 2097168 | tf_op jit(solution)/shard_map/all_gather | solution.py:70
  177.4 11.7 %fusion.92.x_ref = f32[2048,768]{1,0:T(8,128)} fusion(bf16[2048,2048]{1,0:T(8,128)(2,1)} %fusion.2.a_ref, bf16[2048,768]{1,0:T(8,128)(2,1)} %bitcast.360), kind=kOutput, calls=%fused_computation.269 | convolution fusion | flops 6442450944 | bytes 17825792 | tf_op jit(solution)/shard_map/dot_general | solution.py:41
  203.4 25.0 %state_scan.1 = (f32[2048,768]{1,0:T(8,128)}, bf16[8,768,256]{2,1,0:T(8,128)(2,1)S(1)}) custom-call(f32[2048,768]{1,0:T(8,128)} %fusion.92.x_ref, f32[2048,512]{1,0:T(8,128)} %fusion.25.k_ref.r_ref, f32[2048,512]{1,0:T(8,128)} %fusion.25.k_ref.r_ref, f32[2048,128]{1,0:T(8,128)S(1)} %copy.182.col_ref, f32[24,2048]{1,0:T(8,128)S(1)} %select_maximum_fusion.row_ref, ...), custom_call_target="tpu_custom_call" | custom-call | flops 1 | bytes 1 | tf_op jit(solution)/shard_map/state_scan/pallas_call | solution.py:460
  245.8 12.7 %multiply_reduce_fusion.2 = (f32[2048]{0:T(1024)S(1)}, f32[2048,768]{1,0:T(8,128)S(1)}, f32[2048,768]{1,0:T(8,128)}) fusion(f32[2048,768]{1,0:T(8,128)} %get-tuple-element.244.y_ref, bf16[2048,2048]{1,0:T(8,128)(2,1)S(1)} %bitcast.340, bf16[2048,1024]{1,0:T(8,128)(2,1)} %bitcast.354), kind=kOutput, calls=%fused_computation.15 | convolution fusion | flops 6453458944 | bytes 30416896 | tf_op jit(solution)/shard_map/dot_general | solution.py:41
  272.1 19.7 %attend.1 = (bf16[2048,256]{1,0:T(8,128)(2,1)S(1)}, f32[2048,256]{1,0:T(8,128)S(1)}) custom-call(bf16[2048,256]{1,0:T(8,128)(2,1)S(1)} %convolution_convert_fusion.4.q_ref, bf16[2048,512]{1,0:T(8,128)(2,1)} %convolution_convert_fusion.3.k_ref.v_ref, bf16[2048,512]{1,0:T(8,128)(2,1)} %convolution_convert_fusion.3.k_ref.v_ref, f32[2048,128]{1,0:T(8,128)S(1)} %copy-done.3, ...), custom_call_target="tpu_custom_call" | custom-call | flops 1 | bytes 1 | tf_op jit(solution)/shard_map/attend/pallas_call | solution.py:282
  295.8 11.1 %collective-permute-done.26 = bf16[4,256,1024]{2,1,0:T(8,128)(2,1)} collective-permute-done((bf16[4,256,1024]{2,1,0:T(8,128)(2,1)}, bf16[4,256,1024]{2,1,0:T(8,128)(2,1)}, u32[]{:S(2)}, u32[]{:S(2)}) %collective-permute-start.26) | collective-permute-done | bytes 2097184 | tf_op jit(solution)/shard_map/ppermute | solution.py:56
  346.8 35.9 %collective-permute-done.28 = bf16[512,2048]{1,0:T(8,128)(2,1)} collective-permute-done((bf16[512,2048]{1,0:T(8,128)(2,1)S(1)}, bf16[512,2048]{1,0:T(8,128)(2,1)}, u32[]{:S(2)}, u32[]{:S(2)}) %collective-permute-start.28) | collective-permute-done | bytes 2097184 | tf_op jit(solution)/shard_map/ppermute | solution.py:46
  401.7 30.4 %feed_forward.2 = (bf16[1024,2048]{1,0:T(8,128)(2,1)}, bf16[2048,2048]{1,0:T(8,128)(2,1)}, bf16[2048,1024]{1,0:T(8,128)(2,1)}, bf16[2048,1024]{1,0:T(8,128)(2,1)}, bf16[2048,1024]{1,0:T(8,128)(2,1)}) custom-call(bf16[512,2048]{1,0:T(8,128)(2,1)} %copy-done.47, bf16[512,2048]{1,0:T(8,128)(2,1)} %collective-permute-done.32.refs_1_, ...), custom_call_target="tpu_custom_call" | custom-call | flops 1 | bytes 1 | tf_op jit(solution)/shard_map/feed_forward/pallas_call | solution.py:566
  441.3 30.1 %feed_forward.3 = (bf16[1024,2048]{1,0:T(8,128)(2,1)}, bf16[2048,2048]{1,0:T(8,128)(2,1)}, bf16[2048,1024]{1,0:T(8,128)(2,1)}, bf16[2048,1024]{1,0:T(8,128)(2,1)}, bf16[2048,1024]{1,0:T(8,128)(2,1)}) custom-call(bf16[512,2048]{1,0:T(8,128)(2,1)} %collective-permute-done.31.refs_0_, ...), custom_call_target="tpu_custom_call", output_to_operand_aliasing={{1}: (6, {}), {2}: (7, {}), {3}: (8, {}), {4}: (9, {})} | custom-call | flops 1 | bytes 1 | tf_op jit(solution)/shard_map/feed_forward/pallas_call | solution.py:566
  482.3 15.0 %token_sum.8 = bf16[1024,2048]{1,0:T(8,128)(2,1)} custom-call(bf16[2048,1024]{1,0:T(8,128)(2,1)} %get-tuple-element.298.a_ref, bf16[2048,2048]{1,0:T(8,128)(2,1)} %constant_dynamic-update-slice_fusion.refs_2_.b_ref), custom_call_target="tpu_custom_call" | custom-call | flops 1 | bytes 1 | tf_op jit(solution)/shard_map/token_sum/pallas_call | solution.py:602
  497.4 13.3 %token_sum.7 = bf16[2048,1024]{1,0:T(8,128)(2,1)} custom-call(bf16[2048,2048]{1,0:T(8,128)(2,1)} %get-tuple-element.300.a_ref, bf16[2048,1024]{1,0:T(8,128)(2,1)} %get-tuple-element.290.b_ref), custom_call_target="tpu_custom_call" | custom-call | flops 1 | bytes 1 | tf_op jit(solution)/shard_map/token_sum/pallas_call | solution.py:602
  515.0 14.4 %collective-permute-done.37 = bf16[512,2048]{1,0:T(8,128)(2,1)S(1)} collective-permute-done((bf16[512,2048]{1,0:T(8,128)(2,1)}, bf16[512,2048]{1,0:T(8,128)(2,1)S(1)}, u32[]{:S(2)}, u32[]{:S(2)}) %collective-permute-start.37) | collective-permute-done | bytes 2097184 | tf_op jit(solution)/shard_map/ppermute | solution.py:46
  546.7 13.4 %token_sum.9 = bf16[2048,1024]{1,0:T(8,128)(2,1)} custom-call(bf16[2048,2048]{1,0:T(8,128)(2,1)} %get-tuple-element.300.a_ref, bf16[2048,1024]{1,0:T(8,128)(2,1)} %get-tuple-element.301.b_ref), custom_call_target="tpu_custom_call" | custom-call | flops 1 | bytes 1 | tf_op jit(solution)/shard_map/token_sum/pallas_call | solution.py:602
  560.0 12.1 %convolution_convert_fusion = bf16[2048,2048]{1,0:T(8,128)(2,1)S(1)} fusion(bf16[2048,1024]{1,0:T(8,128)(2,1)} %get-tuple-element.298.a_ref, bf16[1024,2048]{1,0:T(8,128)(2,1)} %bitcast.376), kind=kOutput, calls=%fused_computation.9 | convolution fusion | flops 8594128896 | bytes 16777216 | tf_op jit(solution)/shard_map/dot_general | solution.py:41
  572.1 17.6 %collective-permute-done.39.refs_2_ = bf16[512,2048]{1,0:T(8,128)(2,1)} collective-permute-done((bf16[512,2048]{1,0:T(8,128)(2,1)S(1)}, bf16[512,2048]{1,0:T(8,128)(2,1)}, u32[]{:S(2)}, u32[]{:S(2)}) %collective-permute-start.39) | collective-permute-done | bytes 2097184 | tf_op jit(solution)/shard_map/ppermute | solution.py:46
  605.7 8.3 place_rows.3.b_ref
  614.2 15.0 %token_sum.10 = bf16[1024,2048]{1,0:T(8,128)(2,1)} custom-call(bf16[2048,1024]{1,0:T(8,128)(2,1)} %pad_maximum_fusion.1.a_ref, bf16[2048,2048]{1,0:T(8,128)(2,1)} %place_rows.3.b_ref), custom_call_target="tpu_custom_call" | custom-call | flops 1 | bytes 1 | tf_op jit(solution)/shard_map/token_sum/pallas_call | solution.py:602
  634.6 12.8 %fusion.93 = f32[2048,1024]{1,0:T(8,128)S(1)} fusion(bf16[2048,2048]{1,0:T(8,128)(2,1)} %place_rows.3.b_ref, bf16[1024,2048]{1,0:T(8,128)(2,1)} %bitcast.63), kind=kOutput, calls=%fused_computation.270 | convolution fusion | flops 8589934592 | bytes 20971520 | tf_op jit(solution)/shard_map/dot_general | solution.py:41
  656.0 28.5 %attend_back.1 = (f32[2048,256]{1,0:T(8,128)S(1)}, f32[2048,256]{1,0:T(8,128)}, f32[2048,256]{1,0:T(8,128)}) custom-call(bf16[2048,256]{1,0:T(8,128)(2,1)S(1)} %copy-done.10, bf16[2048,512]{1,0:T(8,128)(2,1)} %convolution_convert_fusion.3.k_ref.v_ref, bf16[2048,512]{1,0:T(8,128)(2,1)} %convolution_convert_fusion.3.k_ref.v_ref, f32[2048,128]{1,0:T(8,128)S(1)} %copy-done.4, ...), custom_call_target="tpu_custom_call" | custom-call | flops 1 | bytes 1 | tf_op jit(solution)/shard_map/attend_back/pallas_call | solution.py:300
  693.5 12.7 %fusion.22 = (f32[2048,768]{1,0:T(8,128)}, bf16[2048,768]{1,0:T(8,128)(2,1)S(1)}) fusion(f32[2048]{0:T(1024)S(1)} %add_multiply_fusion.1, f32[2048,768]{1,0:T(8,128)} %copy-done.27, f32[2048,1024]{1,0:T(8,128)} %copy-done.37, f32[768]{0:T(1024)S(1)} %copy-done.87, f32[2048]{0:T(1024)S(1)} %copy-done.81, f32[2048,768]{1,0:T(8,128)} %get-tuple-element.440, ...), kind=kLoop, calls=%fused_computation.67 | loop fusion | flops 26738688 | bytes 34622464 | tf_op jit(solution)/shard_map/mul | solution.py:1171
  708.8 13.4 %token_sum.11 = bf16[2048,1024]{1,0:T(8,128)(2,1)} custom-call(bf16[2048,2048]{1,0:T(8,128)(2,1)} %fusion.2.a_ref, bf16[2048,1024]{1,0:T(8,128)(2,1)} %pad_maximum_fusion.5.b_ref.refs_1_), custom_call_target="tpu_custom_call" | custom-call | flops 1 | bytes 1 | tf_op jit(solution)/shard_map/token_sum/pallas_call | solution.py:602
  733.6 34.1 %state_scan_back.1 = (bf16[2048,768]{1,0:T(8,128)(2,1)}, bf16[2048,256]{1,0:T(8,128)(2,1)S(1)}, bf16[2048,256]{1,0:T(8,128)(2,1)S(1)}, f32[2048,128]{1,0:T(8,128)S(1)}, f32[8,8,768]{2,1,0:T(8,128)S(1)}) custom-call(f32[2048,768]{1,0:T(8,128)} %fusion.92.x_ref, f32[2048,512]{1,0:T(8,128)} %fusion.25.k_ref.r_ref, f32[2048,512]{1,0:T(8,128)} %fusion.25.k_ref.r_ref, ...), custom_call_target="tpu_custom_call" | custom-call | flops 1 | bytes 1 | tf_op jit(solution)/shard_map/state_scan_back/pallas_call | solution.py:496
  775.6 10.9 %token_sum.12 = bf16[2048,768]{1,0:T(8,128)(2,1)} custom-call(bf16[2048,2048]{1,0:T(8,128)(2,1)} %fusion.2.a_ref, bf16[2048,768]{1,0:T(8,128)(2,1)} %get-tuple-element.320.b_ref.refs_0_), custom_call_target="tpu_custom_call" | custom-call | flops 1 | bytes 1 | tf_op jit(solution)/shard_map/token_sum/pallas_call | solution.py:602
  812.8 16.0 %token_sum.13 = bf16[2048,1152]{1,0:T(8,128)(2,1)} custom-call(bf16[2048,2048]{1,0:T(8,128)(2,1)} %fusion.2.a_ref, bf16[2048,1152]{1,0:T(8,128)(2,1)} %pad_dynamic-update-slice_fusion.b_ref.refs_2_), custom_call_target="tpu_custom_call" | custom-call | flops 1 | bytes 1 | tf_op jit(solution)/shard_map/token_sum/pallas_call | solution.py:602
  828.9 19.7 %grad_normed.2 = bf16[1024,2048]{1,0:T(8,128)(2,1)} custom-call(s32[1]{0:T(128)} %bitcast.112.chip_ref, bf16[2048,768]{1,0:T(8,128)(2,1)S(1)} %copy-done.2, bf16[2048,1024]{1,0:T(8,128)(2,1)} %pad_maximum_fusion.5.b_ref.refs_1_, bf16[2048,1152]{1,0:T(8,128)(2,1)} %pad_dynamic-update-slice_fusion.b_ref.refs_2_, bf16[2048,768]{1,0:T(8,128)(2,1)} %bitcast.361, ...), custom_call_target="tpu_custom_call" | custom-call | flops 1 | bytes 1 | tf_op jit(solution)/shard_map/grad_normed/pallas_call | solution.py:635
  896.2 19.9 %grad_normed.3 = bf16[1024,2048]{1,0:T(8,128)(2,1)} custom-call(s32[1]{0:T(128)} %bitcast.126.chip_ref, bf16[2048,768]{1,0:T(8,128)(2,1)S(1)} %copy-done.2, bf16[2048,1024]{1,0:T(8,128)(2,1)} %pad_maximum_fusion.5.b_ref.refs_1_, bf16[2048,1152]{1,0:T(8,128)(2,1)} %pad_dynamic-update-slice_fusion.b_ref.refs_2_, bf16[2048,768]{1,0:T(8,128)(2,1)} %bitcast.362, ...), custom_call_target="tpu_custom_call" | custom-call | flops 1 | bytes 1 | tf_op jit(solution)/shard_map/grad_normed/pallas_call | solution.py:635
  931.6 9.5 collective-permute-done.62
  947.9 27.5 %collective-permute-done.57 = bf16[512,2048]{1,0:T(8,128)(2,1)} collective-permute-done((bf16[512,2048]{1,0:T(8,128)(2,1)}, bf16[512,2048]{1,0:T(8,128)(2,1)}, u32[]{:S(2)}, u32[]{:S(2)}) %collective-permute-start.57) | collective-permute-done | bytes 2097184 | tf_op jit(solution)/shard_map/ppermute | solution.py:46
  (642 shorter events, 432.3 us)
Async XLA Ops:
  7.2 78.0 %all-gather.14.cloned.1.call-start = ((), (), s32[]{:S(2)}) async-start(), calls=%async_computation.15 | async-start | bytes 1966080 | tf_op jit(solution)/shard_map/all_gather | solution.py:70
  14.1 50.2 %collective-permute-start.8 = (bf16[128,2048]{1,0:T(8,128)(2,1)}, bf16[128,2048]{1,0:T(8,128)(2,1)}, u32[]{:S(2)}, u32[]{:S(2)}) collective-permute-start(bf16[128,2048]{1,0:T(8,128)(2,1)} %convert_element_type.319), channel_id=1, source_target_pairs={{4,0},{0,4},{12,8},{8,12},{20,16},{16,20},{28,24},{24,28},{5,1},{1... | collective-permute-start | bytes 1572872 | tf_op jit(solution)/shard_map/ppermute | solution.py:56
  36.6 99.0 %all-gather.16.cloned.1.call-start = ((), (), s32[]{:S(2)}) async-start(), calls=%async_computation.16 | async-start | bytes 2621440 | tf_op jit(solution)/shard_map/all_gather | solution.py:70
  88.6 100.5 %all-gather.18.cloned.1.call-start = ((), (), s32[]{:S(2)}) async-start(), calls=%async_computation.17 | async-start | bytes 2621440 | tf_op jit(solution)/shard_map/all_gather | solution.py:70
  135.6 102.9 %all-gather.20.cloned.1.call-start = ((), (), s32[]{:S(2)}) async-start(), calls=%async_computation.18 | async-start | bytes 2621440 | tf_op jit(solution)/shard_map/all_gather | solution.py:70
  138.9 91.3 %collective-permute-start.18 = (bf16[4,256,1024]{2,1,0:T(8,128)(2,1)}, bf16[4,256,1024]{2,1,0:T(8,128)(2,1)}, u32[]{:S(2)}, u32[]{:S(2)}) collective-permute-start(bf16[4,256,1024]{2,1,0:T(8,128)(2,1)} %bitcast.29), channel_id=1, source_target_pairs={{4,0},{0,4},{12,8},{8,12},{20,16},{16,20},{28,24},{24,28},{5,1},{1... | collective-permute-start | bytes 6291464 | tf_op jit(solution)/shard_map/ppermute | solution.py:56
  177.2 118.6 %all-gather.22.cloned.1.call-start = ((), (), s32[]{:S(2)}) async-start(), calls=%async_computation.19 | async-start | bytes 2621440 | tf_op jit(solution)/shard_map/all_gather | solution.py:70
  189.2 48.5 %collective-permute-start.19 = (bf16[4,128,2048]{2,1,0:T(8,128)(2,1)}, bf16[4,128,2048]{2,1,0:T(8,128)(2,1)}, u32[]{:S(2)}, u32[]{:S(2)}) collective-permute-start(bf16[4,128,2048]{2,1,0:T(8,128)(2,1)} %bitcast.401), channel_id=1, source_target_pairs={{4,0},{0,4},{12,8},{8,12},{20,16},{16,20},{28,24},{24,28},{5,1},{1... | collective-permute-start | bytes 6291464 | tf_op jit(solution)/shard_map/ppermute | solution.py:56
  189.7 48.8 %collective-permute-start.23 = (bf16[512,2048]{1,0:T(8,128)(2,1)}, bf16[512,2048]{1,0:T(8,128)(2,1)}, u32[]{:S(2)}, u32[]{:S(2)}) collective-permute-start(bf16[512,2048]{1,0:T(8,128)(2,1)} %bitcast.378), channel_id=1, source_target_pairs={{2,0},{3,1},{0,2},{1,3},{6,4},{7,5},{4,6},{5,7},{10,8},{11,9},{8,1... | collective-permute-start | bytes 6291464 | tf_op jit(solution)/shard_map/ppermute | solution.py:46
  230.1 171.6 %all-gather.12.cloned.1.call-start = ((), (), s32[]{:S(2)}) async-start(), calls=%async_computation.7 | async-start | bytes 5242880 | tf_op jit(solution)/shard_map/all_gather | solution.py:70
  258.7 48.2 %collective-permute-start.26 = (bf16[4,256,1024]{2,1,0:T(8,128)(2,1)}, bf16[4,256,1024]{2,1,0:T(8,128)(2,1)}, u32[]{:S(2)}, u32[]{:S(2)}) collective-permute-start(bf16[4,256,1024]{2,1,0:T(8,128)(2,1)} %bitcast.56), channel_id=1, source_target_pairs={{4,0},{0,4},{12,8},{8,12},{20,16},{16,20},{28,24},{24,28},{5,1},{1... | collective-permute-start | bytes 6291464 | tf_op jit(solution)/shard_map/ppermute | solution.py:56
  322.1 447.5 %reduce-scatter.14.cloned.1.call-start = ((), (), s32[]{:S(2)}) async-start(), calls=%async_computation.11 | async-start | bytes 5242880 | tf_op jit(solution)/shard_map/reduce_scatter | solution.py:1100
  335.1 47.6 %collective-permute-start.28 = (bf16[512,2048]{1,0:T(8,128)(2,1)S(1)}, bf16[512,2048]{1,0:T(8,128)(2,1)}, u32[]{:S(2)}, u32[]{:S(2)}) collective-permute-start(bf16[512,2048]{1,0:T(8,128)(2,1)S(1)} %fusion.19), channel_id=1, source_target_pairs={{2,0},{3,1},{0,2},{1,3},{6,4},{7,5},{4,6},{5,7},{10,8},{11,9},{8,1... | collective-permute-start | bytes 6291464 | tf_op jit(solution)/shard_map/ppermute | solution.py:46
  336.0 47.5 %collective-permute-start.30 = (bf16[4,256,1024]{2,1,0:T(8,128)(2,1)S(1)}, bf16[4,256,1024]{2,1,0:T(8,128)(2,1)S(1)}, u32[]{:S(2)}, u32[]{:S(2)}) collective-permute-start(bf16[4,256,1024]{2,1,0:T(8,128)(2,1)S(1)} %bitcast.403), channel_id=1, source_target_pairs={{4,0},{0,4},{12,8},{8,12},{20,16},{16,20},{28,24},{24,28},{5,1},{1... | collective-permute-start | bytes 6291464 | tf_op jit(solution)/shard_map/ppermute | solution.py:56
  337.5 52.9 %collective-permute-start.33 = (bf16[512,2048]{1,0:T(8,128)(2,1)S(1)}, bf16[512,2048]{1,0:T(8,128)(2,1)S(1)}, u32[]{:S(2)}, u32[]{:S(2)}) collective-permute-start(bf16[512,2048]{1,0:T(8,128)(2,1)S(1)} %bitcast.379), channel_id=1, source_target_pairs={{1,0},{0,1},{3,2},{2,3},{5,4},{4,5},{7,6},{6,7},{9,8},{8,9},{11,10... | collective-permute-start | bytes 6291464 | tf_op jit(solution)/shard_map/ppermute | solution.py:46
  337.5 57.6 %collective-permute-start.34 = (bf16[512,2048]{1,0:T(8,128)(2,1)}, bf16[512,2048]{1,0:T(8,128)(2,1)S(1)}, u32[]{:S(2)}, u32[]{:S(2)}) collective-permute-start(bf16[512,2048]{1,0:T(8,128)(2,1)} %collective-permute-done.23), channel_id=1, source_target_pairs={{1,0},{0,1},{3,2},{2,3},{5,4},{4,5},{7,6},{6,7},{9,8},{8,9},{11,10... | collective-permute-start | bytes 6291464 | tf_op jit(solution)/shard_map/ppermute | solution.py:46
  387.4 48.1 %collective-permute-start.31 = (bf16[512,2048]{1,0:T(8,128)(2,1)S(1)}, bf16[512,2048]{1,0:T(8,128)(2,1)}, u32[]{:S(2)}, u32[]{:S(2)}) collective-permute-start(bf16[512,2048]{1,0:T(8,128)(2,1)S(1)} %multiply_convert_fusion.2.refs_0_), channel_id=1, source_target_pairs={{2,0},{3,1},{0,2},{1,3},{6,4},{7,5},{4,6},{5,7},{10,8},{11,9},{8,1... | collective-permute-start | bytes 6291464 | tf_op jit(solution)/shard_map/ppermute | solution.py:46
  481.3 48.1 %collective-permute-start.37 = (bf16[512,2048]{1,0:T(8,128)(2,1)}, bf16[512,2048]{1,0:T(8,128)(2,1)S(1)}, u32[]{:S(2)}, u32[]{:S(2)}) collective-permute-start(bf16[512,2048]{1,0:T(8,128)(2,1)} %add_convert_fusion.4), channel_id=1, source_target_pairs={{2,0},{3,1},{0,2},{1,3},{6,4},{7,5},{4,6},{5,7},{10,8},{11,9},{8,1... | collective-permute-start | bytes 6291464 | tf_op jit(solution)/shard_map/ppermute | solution.py:46
  529.5 276.1 %reduce-scatter.8.cloned.1.call-start = ((), (), s32[]{:S(2)}) async-start(), calls=%async_computation.8 | async-start | bytes 2621440 | tf_op jit(solution)/shard_map/reduce_scatter | solution.py:112
  545.3 48.4 %collective-permute-start.41 = (bf16[4,256,1024]{2,1,0:T(8,128)(2,1)}, bf16[4,256,1024]{2,1,0:T(8,128)(2,1)}, u32[]{:S(2)}, u32[]{:S(2)}) collective-permute-start(bf16[4,256,1024]{2,1,0:T(8,128)(2,1)} %get-tuple-element.404), channel_id=1, source_target_pairs={{4,0},{0,4},{12,8},{8,12},{20,16},{16,20},{28,24},{24,28},{5,1},{1... | collective-permute-start | bytes 6291464 | tf_op jit(solution)/shard_map/ppermute | solution.py:56
  596.1 88.4 %collective-permute-start.46 = (bf16[4,256,1024]{2,1,0:T(8,128)(2,1)}, bf16[4,256,1024]{2,1,0:T(8,128)(2,1)}, u32[]{:S(2)}, u32[]{:S(2)}) collective-permute-start(bf16[4,256,1024]{2,1,0:T(8,128)(2,1)} %get-tuple-element.402), channel_id=1, source_target_pairs={{4,0},{0,4},{12,8},{8,12},{20,16},{16,20},{28,24},{24,28},{5,1},{1... | collective-permute-start | bytes 6291464 | tf_op jit(solution)/shard_map/ppermute | solution.py:56
  600.0 51.4 %collective-permute-start.48 = (bf16[512,2048]{1,0:T(8,128)(2,1)}, bf16[512,2048]{1,0:T(8,128)(2,1)}, u32[]{:S(2)}, u32[]{:S(2)}) collective-permute-start(bf16[512,2048]{1,0:T(8,128)(2,1)} %get-tuple-element.397), channel_id=1, source_target_pairs={{1,0},{0,1},{3,2},{2,3},{5,4},{4,5},{7,6},{6,7},{9,8},{8,9},{11,10... | collective-permute-start | bytes 6291464 | tf_op jit(solution)/shard_map/ppermute | solution.py:46
  614.1 191.5 %reduce-scatter.10.cloned.1.call-start = ((), (), s32[]{:S(2)}) async-start(), calls=%async_computation.9 | async-start | bytes 2621440 | tf_op jit(solution)/shard_map/reduce_scatter | solution.py:112
  634.2 55.2 %collective-permute-start.47 = (bf16[4,128,2048]{2,1,0:T(8,128)(2,1)}, bf16[4,128,2048]{2,1,0:T(8,128)(2,1)}, u32[]{:S(2)}, u32[]{:S(2)}) collective-permute-start(bf16[4,128,2048]{2,1,0:T(8,128)(2,1)} %get-tuple-element.400), channel_id=1, source_target_pairs={{4,0},{0,4},{12,8},{8,12},{20,16},{16,20},{28,24},{24,28},{5,1},{1... | collective-permute-start | bytes 6291464 | tf_op jit(solution)/shard_map/ppermute | solution.py:56
  693.3 158.1 %reduce-scatter.12.cloned.1.call-start = ((), (), s32[]{:S(2)}) async-start(), calls=%async_computation.10 | async-start | bytes 2621440 | tf_op jit(solution)/shard_map/reduce_scatter | solution.py:112
  727.0 48.5 %collective-permute-start.49 = (bf16[4,256,1024]{2,1,0:T(8,128)(2,1)}, bf16[4,256,1024]{2,1,0:T(8,128)(2,1)}, u32[]{:S(2)}, u32[]{:S(2)}) collective-permute-start(bf16[4,256,1024]{2,1,0:T(8,128)(2,1)} %get-tuple-element.398), channel_id=1, source_target_pairs={{4,0},{0,4},{12,8},{8,12},{20,16},{16,20},{28,24},{24,28},{5,1},{1... | collective-permute-start | bytes 6291464 | tf_op jit(solution)/shard_map/ppermute | solution.py:56
  728.4 47.2 %collective-permute-start.50 = (bf16[512,2048]{1,0:T(8,128)(2,1)}, bf16[512,2048]{1,0:T(8,128)(2,1)}, u32[]{:S(2)}, u32[]{:S(2)}) collective-permute-start(bf16[512,2048]{1,0:T(8,128)(2,1)} %fusion.15), channel_id=1, source_target_pairs={{2,0},{3,1},{0,2},{1,3},{6,4},{7,5},{4,6},{5,7},{10,8},{11,9},{8,1... | collective-permute-start | bytes 6291464 | tf_op jit(solution)/shard_map/ppermute | solution.py:46
  733.1 183.0 %reduce-scatter.18.cloned.1.call-start = ((), (), s32[]{:S(2)}) async-start(), calls=%async_computation.13 | async-start | bytes 2621440 | tf_op jit(solution)/shard_map/reduce_scatter | solution.py:112
  799.0 117.1 %reduce-scatter.16.cloned.1.call-start = ((), (), s32[]{:S(2)}) async-start(), calls=%async_computation.12 | async-start | bytes 1966080 | tf_op jit(solution)/shard_map/reduce_scatter | solution.py:112
  810.4 61.1 %collective-permute-start.42 = (bf16[512,2048]{1,0:T(8,128)(2,1)}, bf16[512,2048]{1,0:T(8,128)(2,1)}, u32[]{:S(2)}, u32[]{:S(2)}) collective-permute-start(bf16[512,2048]{1,0:T(8,128)(2,1)} %get-tuple-element.396), channel_id=1, source_target_pairs={{1,0},{0,1},{3,2},{2,3},{5,4},{4,5},{7,6},{6,7},{9,8},{8,9},{11,10... | collective-permute-start | bytes 6291464 | tf_op jit(solution)/shard_map/ppermute | solution.py:46
  866.9 108.7 %reduce-scatter.20.cloned.1.call-start = ((), (), s32[]{:S(2)}) async-start(), calls=%async_computation.14 | async-start | bytes 737280 | tf_op jit(solution)/shard_map/reduce_scatter | solution.py:112
  921.0 54.4 %collective-permute-start.57 = (bf16[512,2048]{1,0:T(8,128)(2,1)}, bf16[512,2048]{1,0:T(8,128)(2,1)}, u32[]{:S(2)}, u32[]{:S(2)}) collective-permute-start(bf16[512,2048]{1,0:T(8,128)(2,1)} %fusion.14), channel_id=1, source_target_pairs={{2,0},{3,1},{0,2},{1,3},{6,4},{7,5},{4,6},{5,7},{10,8},{11,9},{8,1... | collective-permute-start | bytes 6291464 | tf_op jit(solution)/shard_map/ppermute | solution.py:46
  (162 other events, 2253.8 us)
Sparse Core Ops, SparseCore 0:
  36.7 38.3 all-gather.13
  88.8 46.7 all-gather.15
  137.7 44.6 all-gather.17
  184.4 44.6 all-gather.19
  231.1 44.6 all-gather.21
  322.3 79.4 all-gather.11
  529.6 75.0 reduce-scatter.13
  614.2 41.2 reduce-scatter.7
  693.4 41.9 reduce-scatter.9
  738.2 43.1 reduce-scatter.11
  799.1 42.6 reduce-scatter.17
  867.0 33.0 reduce-scatter.15
  942.1 20.0 reduce-scatter.19

commit v2 on v1

--- a/solution.py
+++ b/solution.py
@@ -223,27 +223,45 @@
     return min(reach, total_len - QBLOCK), min(reach + QBLOCK, total_len)
 
 
-def attention_scores(total_len, q_ref, k_ref, col_ref, row_ref):
-    back, window = attention_window(total_len)
+def attention_spans(total_len, col_ref, row_ref, body):
+    _, window = attention_window(total_len)
     first = pl.program_id(1) * QBLOCK
-    start = pl.multiple_of(jnp.maximum(first - back, 0), QBLOCK)
-    keys = k_ref[pl.ds(start, window), :]
+    lowest = jnp.min(col_ref[:, 0:1])
+    open_still = first >= 0
+    for size in (2 * QBLOCK, 3 * QBLOCK, window):
+        start = pl.multiple_of(jnp.maximum(first - (size - QBLOCK), 0), QBLOCK)
+        if size < window:
+            before = pl.multiple_of(jnp.maximum(first - size, 0), QBLOCK)
+            highest = jnp.max(row_ref[0:1, pl.ds(before, QBLOCK)])
+            fits = jnp.logical_or(first < size, highest < lowest)
+        else:
+            fits = first >= 0
+        pl.when(jnp.logical_and(open_still, fits))(functools.partial(body, start, size))
+        open_still = jnp.logical_and(open_still, jnp.logical_not(fits))
+
+
+def attention_scores(start, size, q_ref, k_ref, col_ref, row_ref):
+    first = pl.program_id(1) * QBLOCK
+    keys = k_ref[pl.ds(start, size), :]
     scores = dot(q_ref[...], keys, NT) * HD ** (-0.5)
-    query_place = first + lax.broadcasted_iota(jnp.int32, (QBLOCK, window), 0)
-    key_place = start + lax.broadcasted_iota(jnp.int32, (QBLOCK, window), 1)
-    key_seg = row_ref[0:1, pl.ds(start, window)]
+    query_place = first + lax.broadcasted_iota(jnp.int32, (QBLOCK, size), 0)
+    key_place = start + lax.broadcasted_iota(jnp.int32, (QBLOCK, size), 1)
+    key_seg = row_ref[0:1, pl.ds(start, size)]
     allowed = (key_place <= query_place) & (col_ref[:, 0:1] == key_seg)
-    return start, window, keys, jnp.where(allowed, scores, -1e30)
+    return keys, jnp.where(allowed, scores, -1e30)
 
 
 def attend_kernel(total_len, q_ref, k_ref, v_ref, col_ref, row_ref, out_ref, log_ref):
-    start, window, _, scores = attention_scores(total_len, q_ref, k_ref, col_ref, row_ref)
-    peak = jnp.max(scores, axis=1, keepdims=True)
-    expo = jnp.exp(scores - peak)
-    log_total = peak + jnp.log(jnp.sum(expo, axis=1, keepdims=True))
-    shares = jnp.exp(scores - log_total).astype(bf16)
-    out_ref[...] = dot(shares, v_ref[pl.ds(start, window), :]).astype(out_ref.dtype)
-    log_ref[...] = jnp.broadcast_to(log_total, log_ref.shape)
+    def body(start, size):
+        _, scores = attention_scores(start, size, q_ref, k_ref, col_ref, row_ref)
+        peak = jnp.max(scores, axis=1, keepdims=True)
+        expo = jnp.exp(scores - peak)
+        total = jnp.sum(expo, axis=1, keepdims=True)
+        shares = (expo * (1.0 / total)).astype(bf16)
+        out_ref[...] = dot(shares, v_ref[pl.ds(start, size), :]).astype(out_ref.dtype)
+        log_ref[...] = jnp.broadcast_to(peak + jnp.log(total), log_ref.shape)
+
+    attention_spans(total_len, col_ref, row_ref, body)
 
 
 def attend_back_kernel(
@@ -254,17 +272,20 @@
         dk_ref[...] = jnp.zeros_like(dk_ref)
         dv_ref[...] = jnp.zeros_like(dv_ref)
 
-    start, window, keys, scores = attention_scores(total_len, q_ref, k_ref, col_ref, row_ref)
-    shares = jnp.exp(scores - log_ref[:, 0:1])
-    grad = grad_ref[...]
-    grad_shares = dot(grad, v_ref[pl.ds(start, window), :], NT)
-    inner = jnp.sum(shares * grad_shares, axis=1, keepdims=True)
-    grad_scores = (shares * (grad_shares - inner)).astype(bf16)
-    scale = HD ** (-0.5)
-    dq_ref[...] = dot(grad_scores, keys) * scale
-    span = pl.ds(start, window)
-    dk_ref[span, :] += dot(grad_scores, q_ref[...], TN) * scale
-    dv_ref[span, :] += dot(shares.astype(bf16), grad, TN)
+    def body(start, size):
+        keys, scores = attention_scores(start, size, q_ref, k_ref, col_ref, row_ref)
+        shares = jnp.exp(scores - log_ref[:, 0:1])
+        grad = grad_ref[...]
+        grad_shares = dot(grad, v_ref[pl.ds(start, size), :], NT)
+        inner = jnp.sum(shares * grad_shares, axis=1, keepdims=True)
+        grad_scores = (shares * (grad_shares - inner)).astype(bf16)
+        scale = HD ** (-0.5)
+        dq_ref[...] = dot(grad_scores, keys) * scale
+        span = pl.ds(start, size)
+        dk_ref[span, :] += dot(grad_scores, q_ref[...], TN) * scale
+        dv_ref[span, :] += dot(shares.astype(bf16), grad, TN)
+
+    attention_spans(total_len, col_ref, row_ref, body)
 
 
 def attention_specs(total_len, offset):
@@ -1245,7 +1266,7 @@
     for e, rows in {0: near_rows, **far_rows}.items():
         unit = chip_rows(tokens, e).astype(f32) * chip_rows(scale_in, e)
         grad_gain_in += jnp.sum(rows.reshape(2 * length, D).astype(f32) * unit, axis=0)
-    got, near, grad_gain_in = fence(got, near, grad_gain_in)
+    got, near = fence(got, near)
 
     sum_own = jnp.concatenate([sum_streams, sum_qz], axis=1)
     got_own = exchange_ctx(by_distance(sum_own.reshape(peers, in_rows, own_width)))

time: 1020 us -> 1020 us (level)
  transfers between devices with their start and end apart: 84 -> 84, of which waited for: 33 -> 33; matrix products, arithmetic and copies ran while one was open for 33% -> 34% of each run, Pallas kernels for 30% -> 30%
where the time goes in v2:
time: 1020 us; the launch traced here: 1010 us
  Pallas kernels  329 us (32%)
  waiting for transfers between devices  224 us (22%)
  other arithmetic  160 us (16%)
  local copies, waits for them, and re-layouts  136 us (13%)
  matrix products  85.3 us (8%)
  starting transfers between devices  56.9 us (6%)
  between operations  16 us (2%)
    ppermute x51, waiting for transfers between devices, from_ctx(): return lax.ppermute(x, 'ctx', [(i ^ m, i) for i in range(count)])  139 us
    pallas_call x7, Pallas kernels, token_sum(): pl.pallas_call(token_sum_kernel, grid=(rows // tile,), in_specs=[pl.Block...  97.3 us
    dot_general x10, matrix products, dot(): return lax.dot_general(a, b, dims, preferred_element_type=f32)  84 us
    pallas_call x2, Pallas kernels, feed_call(): pl.pallas_call(functools.partial(feed_kernel, per_block), grid=(tiles,),...  60.7 us
    ppermute x17, waiting for transfers between devices, from_dp(): return lax.ppermute(x, 'dp', pairs)  58.4 us
    pallas_call x2, Pallas kernels, normed_call(): pl.pallas_call(normed_kernel, grid_spec=pltpu.PrefetchScalarGridSpec(num_...  39.7 us
    pallas_call x1, Pallas kernels, scan_back_call(): pl.pallas_call(functools.partial(scan_back_kernel, width // 128), grid=(c...  34.1 us
    ppermute x51, starting transfers between devices, from_ctx(): return lax.ppermute(x, 'ctx', [(i ^ m, i) for i in range(count)])  30.4 us
  transfers between devices with their start and end apart: 84, of which 33 were waited for; matrix products, arithmetic and copies ran while one was open for 34% of the time, Pallas kernels for 30%

profile of v2, /device:TPU:0, one launch (start us, length us, event | category | flops | bytes accessed | tf_op | source)
XLA Modules:
  0.0 1007.0 jit_solution(15651187765793478286)
XLA Ops:
  50.8 13.4 %collective-permute-done.7 = bf16[4,64,1152]{2,1,0:T(8,128)(2,1)S(1)} collective-permute-done((bf16[4,64,1152]{2,1,0:T(8,128)(2,1)S(1)}, bf16[4,64,1152]{2,1,0:T(8,128)(2,1)S(1)}, u32[]{:S(2)}, u32[]{:S(2)}) %collective-permute-start.7) | collective-permute-done | bytes 589856 | tf_op jit(solution)/shard_map/ppermute | solution.py:56
  64.3 20.9 %collective-permute-done.3.refs_2_ = bf16[512,2048]{1,0:T(8,128)(2,1)} collective-permute-done((bf16[512,2048]{1,0:T(8,128)(2,1)S(1)}, bf16[512,2048]{1,0:T(8,128)(2,1)}, u32[]{:S(2)}, u32[]{:S(2)}) %collective-permute-start.3) | collective-permute-done | bytes 2097184 | tf_op jit(solution)/shard_map/ppermute | solution.py:46
  92.7 9.8 place_rows.2
  107.7 8.8 fusion.2.a_ref
  116.5 19.1 %all-gather.16.cloned.1.call-done = bf16[1024,1024]{1,0:T(8,128)(2,1)} async-done(((bf16[256,1024]{1,0:T(8,128)(2,1)}), bf16[1024,1024]{1,0:T(8,128)(2,1)}) %all-gather.16.cloned.1.call-update) | async-done | bytes 2097168 | tf_op jit(solution)/shard_map/all_gather | solution.py:70
  177.5 11.7 %fusion.92.x_ref = f32[2048,768]{1,0:T(8,128)} fusion(bf16[2048,2048]{1,0:T(8,128)(2,1)} %fusion.2.a_ref, bf16[2048,768]{1,0:T(8,128)(2,1)} %bitcast.362), kind=kOutput, calls=%fused_computation.269 | convolution fusion | flops 6442450944 | bytes 17825792 | tf_op jit(solution)/shard_map/dot_general | solution.py:41
  203.4 25.0 %state_scan.1 = (f32[2048,768]{1,0:T(8,128)}, bf16[8,768,256]{2,1,0:T(8,128)(2,1)S(1)}) custom-call(f32[2048,768]{1,0:T(8,128)} %fusion.92.x_ref, f32[2048,512]{1,0:T(8,128)} %fusion.25.k_ref.r_ref, f32[2048,512]{1,0:T(8,128)} %fusion.25.k_ref.r_ref, f32[2048,128]{1,0:T(8,128)S(1)} %copy.182.col_ref, f32[24,2048]{1,0:T(8,128)S(1)} %select_maximum_fusion.row_ref, ...), custom_call_target="tpu_custom_call" | custom-call | flops 1 | bytes 1 | tf_op jit(solution)/shard_map/state_scan/pallas_call | solution.py:481
  245.8 12.3 %multiply_reduce_fusion.2 = (f32[2048]{0:T(1024)S(1)}, f32[2048,768]{1,0:T(8,128)S(1)}, f32[2048,768]{1,0:T(8,128)}) fusion(f32[2048,768]{1,0:T(8,128)} %get-tuple-element.243.y_ref, bf16[2048,2048]{1,0:T(8,128)(2,1)S(1)} %bitcast.342, bf16[2048,1024]{1,0:T(8,128)(2,1)} %bitcast.356), kind=kOutput, calls=%fused_computation.15 | convolution fusion | flops 6453458944 | bytes 30416896 | tf_op jit(solution)/shard_map/dot_general | solution.py:41
  271.7 18.5 %attend.1 = (bf16[2048,256]{1,0:T(8,128)(2,1)S(1)}, f32[2048,256]{1,0:T(8,128)S(1)}) custom-call(bf16[2048,256]{1,0:T(8,128)(2,1)S(1)} %convolution_convert_fusion.4.q_ref, bf16[2048,512]{1,0:T(8,128)(2,1)} %convolution_convert_fusion.3.k_ref.v_ref, bf16[2048,512]{1,0:T(8,128)(2,1)} %convolution_convert_fusion.3.k_ref.v_ref, f32[2048,128]{1,0:T(8,128)S(1)} %copy-done.3, ...), custom_call_target="tpu_custom_call" | custom-call | flops 1 | bytes 1 | tf_op jit(solution)/shard_map/attend/pallas_call | solution.py:303
  294.1 12.4 %collective-permute-done.26 = bf16[4,256,1024]{2,1,0:T(8,128)(2,1)} collective-permute-done((bf16[4,256,1024]{2,1,0:T(8,128)(2,1)}, bf16[4,256,1024]{2,1,0:T(8,128)(2,1)}, u32[]{:S(2)}, u32[]{:S(2)}) %collective-permute-start.26) | collective-permute-done | bytes 2097184 | tf_op jit(solution)/shard_map/ppermute | solution.py:56
  346.2 36.0 %collective-permute-done.28 = bf16[512,2048]{1,0:T(8,128)(2,1)} collective-permute-done((bf16[512,2048]{1,0:T(8,128)(2,1)S(1)}, bf16[512,2048]{1,0:T(8,128)(2,1)}, u32[]{:S(2)}, u32[]{:S(2)}) %collective-permute-start.28) | collective-permute-done | bytes 2097184 | tf_op jit(solution)/shard_map/ppermute | solution.py:46
  401.3 30.6 %feed_forward.2 = (bf16[1024,2048]{1,0:T(8,128)(2,1)}, bf16[2048,2048]{1,0:T(8,128)(2,1)}, bf16[2048,1024]{1,0:T(8,128)(2,1)}, bf16[2048,1024]{1,0:T(8,128)(2,1)}, bf16[2048,1024]{1,0:T(8,128)(2,1)}) custom-call(bf16[512,2048]{1,0:T(8,128)(2,1)} %copy-done.45, bf16[512,2048]{1,0:T(8,128)(2,1)} %collective-permute-done.32.refs_1_, ...), custom_call_target="tpu_custom_call" | custom-call | flops 1 | bytes 1 | tf_op jit(solution)/shard_map/feed_forward/pallas_call | solution.py:587
  440.7 30.1 %feed_forward.3 = (bf16[1024,2048]{1,0:T(8,128)(2,1)}, bf16[2048,2048]{1,0:T(8,128)(2,1)}, bf16[2048,1024]{1,0:T(8,128)(2,1)}, bf16[2048,1024]{1,0:T(8,128)(2,1)}, bf16[2048,1024]{1,0:T(8,128)(2,1)}) custom-call(bf16[512,2048]{1,0:T(8,128)(2,1)} %collective-permute-done.31.refs_0_, ...), custom_call_target="tpu_custom_call", output_to_operand_aliasing={{1}: (6, {}), {2}: (7, {}), {3}: (8, {}), {4}: (9, {})} | custom-call | flops 1 | bytes 1 | tf_op jit(solution)/shard_map/feed_forward/pallas_call | solution.py:587
  481.8 14.7 %token_sum.8 = bf16[1024,2048]{1,0:T(8,128)(2,1)} custom-call(bf16[2048,1024]{1,0:T(8,128)(2,1)} %get-tuple-element.297.a_ref, bf16[2048,2048]{1,0:T(8,128)(2,1)} %constant_dynamic-update-slice_fusion.refs_2_.b_ref), custom_call_target="tpu_custom_call" | custom-call | flops 1 | bytes 1 | tf_op jit(solution)/shard_map/token_sum/pallas_call | solution.py:623
  496.5 13.3 %token_sum.7 = bf16[2048,1024]{1,0:T(8,128)(2,1)} custom-call(bf16[2048,2048]{1,0:T(8,128)(2,1)} %get-tuple-element.299.a_ref, bf16[2048,1024]{1,0:T(8,128)(2,1)} %get-tuple-element.289.b_ref), custom_call_target="tpu_custom_call" | custom-call | flops 1 | bytes 1 | tf_op jit(solution)/shard_map/token_sum/pallas_call | solution.py:623
  514.2 14.6 %collective-permute-done.37 = bf16[512,2048]{1,0:T(8,128)(2,1)S(1)} collective-permute-done((bf16[512,2048]{1,0:T(8,128)(2,1)}, bf16[512,2048]{1,0:T(8,128)(2,1)S(1)}, u32[]{:S(2)}, u32[]{:S(2)}) %collective-permute-start.37) | collective-permute-done | bytes 2097184 | tf_op jit(solution)/shard_map/ppermute | solution.py:46
  546.3 13.4 %token_sum.9 = bf16[2048,1024]{1,0:T(8,128)(2,1)} custom-call(bf16[2048,2048]{1,0:T(8,128)(2,1)} %get-tuple-element.299.a_ref, bf16[2048,1024]{1,0:T(8,128)(2,1)} %get-tuple-element.300.b_ref), custom_call_target="tpu_custom_call" | custom-call | flops 1 | bytes 1 | tf_op jit(solution)/shard_map/token_sum/pallas_call | solution.py:623
  559.7 12.1 %convolution_convert_fusion = bf16[2048,2048]{1,0:T(8,128)(2,1)S(1)} fusion(bf16[2048,1024]{1,0:T(8,128)(2,1)} %get-tuple-element.297.a_ref, bf16[1024,2048]{1,0:T(8,128)(2,1)} %bitcast.378), kind=kOutput, calls=%fused_computation.9 | convolution fusion | flops 8594128896 | bytes 16777216 | tf_op jit(solution)/shard_map/dot_general | solution.py:41
  571.8 17.4 %collective-permute-done.39.refs_2_ = bf16[512,2048]{1,0:T(8,128)(2,1)} collective-permute-done((bf16[512,2048]{1,0:T(8,128)(2,1)S(1)}, bf16[512,2048]{1,0:T(8,128)(2,1)}, u32[]{:S(2)}, u32[]{:S(2)}) %collective-permute-start.39) | collective-permute-done | bytes 2097184 | tf_op jit(solution)/shard_map/ppermute | solution.py:46
  605.3 8.4 place_rows.3.b_ref
  613.8 15.3 %token_sum.10 = bf16[1024,2048]{1,0:T(8,128)(2,1)} custom-call(bf16[2048,1024]{1,0:T(8,128)(2,1)} %pad_maximum_fusion.1.a_ref, bf16[2048,2048]{1,0:T(8,128)(2,1)} %place_rows.3.b_ref), custom_call_target="tpu_custom_call" | custom-call | flops 1 | bytes 1 | tf_op jit(solution)/shard_map/token_sum/pallas_call | solution.py:623
  634.3 12.8 %fusion.93 = f32[2048,1024]{1,0:T(8,128)S(1)} fusion(bf16[2048,2048]{1,0:T(8,128)(2,1)} %place_rows.3.b_ref, bf16[1024,2048]{1,0:T(8,128)(2,1)} %bitcast.63), kind=kOutput, calls=%fused_computation.270 | convolution fusion | flops 8589934592 | bytes 20971520 | tf_op jit(solution)/shard_map/dot_general | solution.py:41
  655.8 24.5 %attend_back.1 = (f32[2048,256]{1,0:T(8,128)S(1)}, f32[2048,256]{1,0:T(8,128)}, f32[2048,256]{1,0:T(8,128)}) custom-call(bf16[2048,256]{1,0:T(8,128)(2,1)S(1)} %copy-done.10, bf16[2048,512]{1,0:T(8,128)(2,1)} %convolution_convert_fusion.3.k_ref.v_ref, bf16[2048,512]{1,0:T(8,128)(2,1)} %convolution_convert_fusion.3.k_ref.v_ref, f32[2048,128]{1,0:T(8,128)S(1)} %copy-done.4, ...), custom_call_target="tpu_custom_call" | custom-call | flops 1 | bytes 1 | tf_op jit(solution)/shard_map/attend_back/pallas_call | solution.py:321
  680.4 8.6 collective-permute-done.47
  693.0 12.3 %fusion.22 = (f32[2048,768]{1,0:T(8,128)}, bf16[2048,768]{1,0:T(8,128)(2,1)S(1)}) fusion(f32[2048]{0:T(1024)S(1)} %add_multiply_fusion.1, f32[2048,768]{1,0:T(8,128)} %copy-done.26, f32[2048,1024]{1,0:T(8,128)} %copy-done.35, f32[768]{0:T(1024)S(1)} %copy-done.87, f32[2048]{0:T(1024)S(1)} %copy-done.82, f32[2048,768]{1,0:T(8,128)} %get-tuple-element.438, ...), kind=kLoop, calls=%fused_computation.67 | loop fusion | flops 26738688 | bytes 34622464 | tf_op jit(solution)/shard_map/mul | solution.py:1192
  708.0 13.4 %token_sum.11 = bf16[2048,1024]{1,0:T(8,128)(2,1)} custom-call(bf16[2048,2048]{1,0:T(8,128)(2,1)} %fusion.2.a_ref, bf16[2048,1024]{1,0:T(8,128)(2,1)} %pad_maximum_fusion.5.b_ref.refs_1_), custom_call_target="tpu_custom_call" | custom-call | flops 1 | bytes 1 | tf_op jit(solution)/shard_map/token_sum/pallas_call | solution.py:623
  732.7 34.1 %state_scan_back.1 = (bf16[2048,768]{1,0:T(8,128)(2,1)}, bf16[2048,256]{1,0:T(8,128)(2,1)S(1)}, bf16[2048,256]{1,0:T(8,128)(2,1)S(1)}, f32[2048,128]{1,0:T(8,128)S(1)}, f32[8,8,768]{2,1,0:T(8,128)S(1)}) custom-call(f32[2048,768]{1,0:T(8,128)} %fusion.92.x_ref, f32[2048,512]{1,0:T(8,128)} %fusion.25.k_ref.r_ref, f32[2048,512]{1,0:T(8,128)} %fusion.25.k_ref.r_ref, ...), custom_call_target="tpu_custom_call" | custom-call | flops 1 | bytes 1 | tf_op jit(solution)/shard_map/state_scan_back/pallas_call | solution.py:517
  774.8 10.9 %token_sum.12 = bf16[2048,768]{1,0:T(8,128)(2,1)} custom-call(bf16[2048,2048]{1,0:T(8,128)(2,1)} %fusion.2.a_ref, bf16[2048,768]{1,0:T(8,128)(2,1)} %get-tuple-element.319.b_ref.refs_0_), custom_call_target="tpu_custom_call" | custom-call | flops 1 | bytes 1 | tf_op jit(solution)/shard_map/token_sum/pallas_call | solution.py:623
  811.9 16.3 %token_sum.13 = bf16[2048,1152]{1,0:T(8,128)(2,1)} custom-call(bf16[2048,2048]{1,0:T(8,128)(2,1)} %fusion.2.a_ref, bf16[2048,1152]{1,0:T(8,128)(2,1)} %pad_dynamic-update-slice_fusion.b_ref.refs_2_), custom_call_target="tpu_custom_call" | custom-call | flops 1 | bytes 1 | tf_op jit(solution)/shard_map/token_sum/pallas_call | solution.py:623
  828.3 19.8 %grad_normed.2 = bf16[1024,2048]{1,0:T(8,128)(2,1)} custom-call(s32[1]{0:T(128)} %bitcast.112.chip_ref, bf16[2048,768]{1,0:T(8,128)(2,1)S(1)} %copy-done.2, bf16[2048,1024]{1,0:T(8,128)(2,1)} %pad_maximum_fusion.5.b_ref.refs_1_, bf16[2048,1152]{1,0:T(8,128)(2,1)} %pad_dynamic-update-slice_fusion.b_ref.refs_2_, bf16[2048,768]{1,0:T(8,128)(2,1)} %bitcast.363, ...), custom_call_target="tpu_custom_call" | custom-call | flops 1 | bytes 1 | tf_op jit(solution)/shard_map/grad_normed/pallas_call | solution.py:656
  894.2 19.9 %grad_normed.3 = bf16[1024,2048]{1,0:T(8,128)(2,1)} custom-call(s32[1]{0:T(128)} %bitcast.126.chip_ref, bf16[2048,768]{1,0:T(8,128)(2,1)S(1)} %copy-done.2, bf16[2048,1024]{1,0:T(8,128)(2,1)} %pad_maximum_fusion.5.b_ref.refs_1_, bf16[2048,1152]{1,0:T(8,128)(2,1)} %pad_dynamic-update-slice_fusion.b_ref.refs_2_, bf16[2048,768]{1,0:T(8,128)(2,1)} %bitcast.364, ...), custom_call_target="tpu_custom_call" | custom-call | flops 1 | bytes 1 | tf_op jit(solution)/shard_map/grad_normed/pallas_call | solution.py:656
  977.6 14.8 %collective-permute-done.57 = bf16[512,2048]{1,0:T(8,128)(2,1)} collective-permute-done((bf16[512,2048]{1,0:T(8,128)(2,1)}, bf16[512,2048]{1,0:T(8,128)(2,1)}, u32[]{:S(2)}, u32[]{:S(2)}) %collective-permute-start.57) | collective-permute-done | bytes 2097184 | tf_op jit(solution)/shard_map/ppermute | solution.py:46
  (643 shorter events, 446.0 us)
Async XLA Ops:
  7.2 78.0 %all-gather.14.cloned.1.call-start = ((), (), s32[]{:S(2)}) async-start(), calls=%async_computation.15 | async-start | bytes 1966080 | tf_op jit(solution)/shard_map/all_gather | solution.py:70
  14.1 50.2 %collective-permute-start.8 = (bf16[128,2048]{1,0:T(8,128)(2,1)}, bf16[128,2048]{1,0:T(8,128)(2,1)}, u32[]{:S(2)}, u32[]{:S(2)}) collective-permute-start(bf16[128,2048]{1,0:T(8,128)(2,1)} %convert_element_type.319), channel_id=1, source_target_pairs={{4,0},{0,4},{12,8},{8,12},{20,16},{16,20},{28,24},{24,28},{5,1},{1... | collective-permute-start | bytes 1572872 | tf_op jit(solution)/shard_map/ppermute | solution.py:56
  36.6 99.0 %all-gather.16.cloned.1.call-start = ((), (), s32[]{:S(2)}) async-start(), calls=%async_computation.16 | async-start | bytes 2621440 | tf_op jit(solution)/shard_map/all_gather | solution.py:70
  88.6 100.6 %all-gather.18.cloned.1.call-start = ((), (), s32[]{:S(2)}) async-start(), calls=%async_computation.17 | async-start | bytes 2621440 | tf_op jit(solution)/shard_map/all_gather | solution.py:70
  135.6 102.9 %all-gather.20.cloned.1.call-start = ((), (), s32[]{:S(2)}) async-start(), calls=%async_computation.18 | async-start | bytes 2621440 | tf_op jit(solution)/shard_map/all_gather | solution.py:70
  138.9 91.7 %collective-permute-start.18 = (bf16[4,256,1024]{2,1,0:T(8,128)(2,1)}, bf16[4,256,1024]{2,1,0:T(8,128)(2,1)}, u32[]{:S(2)}, u32[]{:S(2)}) collective-permute-start(bf16[4,256,1024]{2,1,0:T(8,128)(2,1)} %bitcast.29), channel_id=1, source_target_pairs={{4,0},{0,4},{12,8},{8,12},{20,16},{16,20},{28,24},{24,28},{5,1},{1... | collective-permute-start | bytes 6291464 | tf_op jit(solution)/shard_map/ppermute | solution.py:56
  177.2 116.9 %all-gather.22.cloned.1.call-start = ((), (), s32[]{:S(2)}) async-start(), calls=%async_computation.19 | async-start | bytes 2621440 | tf_op jit(solution)/shard_map/all_gather | solution.py:70
  189.2 48.5 %collective-permute-start.19 = (bf16[4,128,2048]{2,1,0:T(8,128)(2,1)}, bf16[4,128,2048]{2,1,0:T(8,128)(2,1)}, u32[]{:S(2)}, u32[]{:S(2)}) collective-permute-start(bf16[4,128,2048]{2,1,0:T(8,128)(2,1)} %bitcast.403), channel_id=1, source_target_pairs={{4,0},{0,4},{12,8},{8,12},{20,16},{16,20},{28,24},{24,28},{5,1},{1... | collective-permute-start | bytes 6291464 | tf_op jit(solution)/shard_map/ppermute | solution.py:56
  189.7 48.8 %collective-permute-start.23 = (bf16[512,2048]{1,0:T(8,128)(2,1)}, bf16[512,2048]{1,0:T(8,128)(2,1)}, u32[]{:S(2)}, u32[]{:S(2)}) collective-permute-start(bf16[512,2048]{1,0:T(8,128)(2,1)} %bitcast.380), channel_id=1, source_target_pairs={{2,0},{3,1},{0,2},{1,3},{6,4},{7,5},{4,6},{5,7},{10,8},{11,9},{8,1... | collective-permute-start | bytes 6291464 | tf_op jit(solution)/shard_map/ppermute | solution.py:46
  230.1 171.2 %all-gather.12.cloned.1.call-start = ((), (), s32[]{:S(2)}) async-start(), calls=%async_computation.7 | async-start | bytes 5242880 | tf_op jit(solution)/shard_map/all_gather | solution.py:70
  258.2 48.2 %collective-permute-start.26 = (bf16[4,256,1024]{2,1,0:T(8,128)(2,1)}, bf16[4,256,1024]{2,1,0:T(8,128)(2,1)}, u32[]{:S(2)}, u32[]{:S(2)}) collective-permute-start(bf16[4,256,1024]{2,1,0:T(8,128)(2,1)} %bitcast.56), channel_id=1, source_target_pairs={{4,0},{0,4},{12,8},{8,12},{20,16},{16,20},{28,24},{24,28},{5,1},{1... | collective-permute-start | bytes 6291464 | tf_op jit(solution)/shard_map/ppermute | solution.py:56
  321.7 447.0 %reduce-scatter.14.cloned.1.call-start = ((), (), s32[]{:S(2)}) async-start(), calls=%async_computation.11 | async-start | bytes 5242880 | tf_op jit(solution)/shard_map/reduce_scatter | solution.py:1121
  334.5 47.8 %collective-permute-start.28 = (bf16[512,2048]{1,0:T(8,128)(2,1)S(1)}, bf16[512,2048]{1,0:T(8,128)(2,1)}, u32[]{:S(2)}, u32[]{:S(2)}) collective-permute-start(bf16[512,2048]{1,0:T(8,128)(2,1)S(1)} %fusion.19), channel_id=1, source_target_pairs={{2,0},{3,1},{0,2},{1,3},{6,4},{7,5},{4,6},{5,7},{10,8},{11,9},{8,1... | collective-permute-start | bytes 6291464 | tf_op jit(solution)/shard_map/ppermute | solution.py:46
  335.4 47.4 %collective-permute-start.30 = (bf16[4,256,1024]{2,1,0:T(8,128)(2,1)S(1)}, bf16[4,256,1024]{2,1,0:T(8,128)(2,1)S(1)}, u32[]{:S(2)}, u32[]{:S(2)}) collective-permute-start(bf16[4,256,1024]{2,1,0:T(8,128)(2,1)S(1)} %bitcast.405), channel_id=1, source_target_pairs={{4,0},{0,4},{12,8},{8,12},{20,16},{16,20},{28,24},{24,28},{5,1},{1... | collective-permute-start | bytes 6291464 | tf_op jit(solution)/shard_map/ppermute | solution.py:56
  336.9 52.8 %collective-permute-start.33 = (bf16[512,2048]{1,0:T(8,128)(2,1)S(1)}, bf16[512,2048]{1,0:T(8,128)(2,1)S(1)}, u32[]{:S(2)}, u32[]{:S(2)}) collective-permute-start(bf16[512,2048]{1,0:T(8,128)(2,1)S(1)} %bitcast.381), channel_id=1, source_target_pairs={{1,0},{0,1},{3,2},{2,3},{5,4},{4,5},{7,6},{6,7},{9,8},{8,9},{11,10... | collective-permute-start | bytes 6291464 | tf_op jit(solution)/shard_map/ppermute | solution.py:46
  336.9 57.5 %collective-permute-start.34 = (bf16[512,2048]{1,0:T(8,128)(2,1)}, bf16[512,2048]{1,0:T(8,128)(2,1)S(1)}, u32[]{:S(2)}, u32[]{:S(2)}) collective-permute-start(bf16[512,2048]{1,0:T(8,128)(2,1)} %collective-permute-done.23), channel_id=1, source_target_pairs={{1,0},{0,1},{3,2},{2,3},{5,4},{4,5},{7,6},{6,7},{9,8},{8,9},{11,10... | collective-permute-start | bytes 6291464 | tf_op jit(solution)/shard_map/ppermute | solution.py:46
  386.8 48.1 %collective-permute-start.31 = (bf16[512,2048]{1,0:T(8,128)(2,1)S(1)}, bf16[512,2048]{1,0:T(8,128)(2,1)}, u32[]{:S(2)}, u32[]{:S(2)}) collective-permute-start(bf16[512,2048]{1,0:T(8,128)(2,1)S(1)} %multiply_convert_fusion.2.refs_0_), channel_id=1, source_target_pairs={{2,0},{3,1},{0,2},{1,3},{6,4},{7,5},{4,6},{5,7},{10,8},{11,9},{8,1... | collective-permute-start | bytes 6291464 | tf_op jit(solution)/shard_map/ppermute | solution.py:46
  480.7 48.1 %collective-permute-start.37 = (bf16[512,2048]{1,0:T(8,128)(2,1)}, bf16[512,2048]{1,0:T(8,128)(2,1)S(1)}, u32[]{:S(2)}, u32[]{:S(2)}) collective-permute-start(bf16[512,2048]{1,0:T(8,128)(2,1)} %add_convert_fusion.4), channel_id=1, source_target_pairs={{2,0},{3,1},{0,2},{1,3},{6,4},{7,5},{4,6},{5,7},{10,8},{11,9},{8,1... | collective-permute-start | bytes 6291464 | tf_op jit(solution)/shard_map/ppermute | solution.py:46
  528.8 276.0 %reduce-scatter.8.cloned.1.call-start = ((), (), s32[]{:S(2)}) async-start(), calls=%async_computation.8 | async-start | bytes 2621440 | tf_op jit(solution)/shard_map/reduce_scatter | solution.py:112
  544.9 48.4 %collective-permute-start.41 = (bf16[4,256,1024]{2,1,0:T(8,128)(2,1)}, bf16[4,256,1024]{2,1,0:T(8,128)(2,1)}, u32[]{:S(2)}, u32[]{:S(2)}) collective-permute-start(bf16[4,256,1024]{2,1,0:T(8,128)(2,1)} %get-tuple-element.402), channel_id=1, source_target_pairs={{4,0},{0,4},{12,8},{8,12},{20,16},{16,20},{28,24},{24,28},{5,1},{1... | collective-permute-start | bytes 6291464 | tf_op jit(solution)/shard_map/ppermute | solution.py:56
  595.6 84.7 %collective-permute-start.46 = (bf16[4,256,1024]{2,1,0:T(8,128)(2,1)}, bf16[4,256,1024]{2,1,0:T(8,128)(2,1)}, u32[]{:S(2)}, u32[]{:S(2)}) collective-permute-start(bf16[4,256,1024]{2,1,0:T(8,128)(2,1)} %get-tuple-element.400), channel_id=1, source_target_pairs={{4,0},{0,4},{12,8},{8,12},{20,16},{16,20},{28,24},{24,28},{5,1},{1... | collective-permute-start | bytes 6291464 | tf_op jit(solution)/shard_map/ppermute | solution.py:56
  599.6 51.6 %collective-permute-start.48 = (bf16[512,2048]{1,0:T(8,128)(2,1)}, bf16[512,2048]{1,0:T(8,128)(2,1)}, u32[]{:S(2)}, u32[]{:S(2)}) collective-permute-start(bf16[512,2048]{1,0:T(8,128)(2,1)} %get-tuple-element.395), channel_id=1, source_target_pairs={{1,0},{0,1},{3,2},{2,3},{5,4},{4,5},{7,6},{6,7},{9,8},{8,9},{11,10... | collective-permute-start | bytes 6291464 | tf_op jit(solution)/shard_map/ppermute | solution.py:46
  613.7 191.1 %reduce-scatter.10.cloned.1.call-start = ((), (), s32[]{:S(2)}) async-start(), calls=%async_computation.9 | async-start | bytes 2621440 | tf_op jit(solution)/shard_map/reduce_scatter | solution.py:112
  634.0 54.9 %collective-permute-start.47 = (bf16[4,128,2048]{2,1,0:T(8,128)(2,1)}, bf16[4,128,2048]{2,1,0:T(8,128)(2,1)}, u32[]{:S(2)}, u32[]{:S(2)}) collective-permute-start(bf16[4,128,2048]{2,1,0:T(8,128)(2,1)} %get-tuple-element.398), channel_id=1, source_target_pairs={{4,0},{0,4},{12,8},{8,12},{20,16},{16,20},{28,24},{24,28},{5,1},{1... | collective-permute-start | bytes 6291464 | tf_op jit(solution)/shard_map/ppermute | solution.py:56
  692.9 159.0 %reduce-scatter.12.cloned.1.call-start = ((), (), s32[]{:S(2)}) async-start(), calls=%async_computation.10 | async-start | bytes 2621440 | tf_op jit(solution)/shard_map/reduce_scatter | solution.py:112
  726.2 48.3 %collective-permute-start.49 = (bf16[4,256,1024]{2,1,0:T(8,128)(2,1)}, bf16[4,256,1024]{2,1,0:T(8,128)(2,1)}, u32[]{:S(2)}, u32[]{:S(2)}) collective-permute-start(bf16[4,256,1024]{2,1,0:T(8,128)(2,1)} %get-tuple-element.396), channel_id=1, source_target_pairs={{4,0},{0,4},{12,8},{8,12},{20,16},{16,20},{28,24},{24,28},{5,1},{1... | collective-permute-start | bytes 6291464 | tf_op jit(solution)/shard_map/ppermute | solution.py:56
  732.2 190.8 %reduce-scatter.18.cloned.1.call-start = ((), (), s32[]{:S(2)}) async-start(), calls=%async_computation.13 | async-start | bytes 2621440 | tf_op jit(solution)/shard_map/reduce_scatter | solution.py:112
  798.1 124.9 %reduce-scatter.16.cloned.1.call-start = ((), (), s32[]{:S(2)}) async-start(), calls=%async_computation.12 | async-start | bytes 1966080 | tf_op jit(solution)/shard_map/reduce_scatter | solution.py:112
  806.7 47.4 %collective-permute-start.51 = (bf16[4,256,768]{2,1,0:T(8,128)(2,1)}, bf16[4,256,768]{2,1,0:T(8,128)(2,1)}, u32[]{:S(2)}, u32[]{:S(2)}) collective-permute-start(bf16[4,256,768]{2,1,0:T(8,128)(2,1)} %get-tuple-element.404), channel_id=1, source_target_pairs={{4,0},{0,4},{12,8},{8,12},{20,16},{16,20},{28,24},{24,28},{5,1},{1... | collective-permute-start | bytes 4718600 | tf_op jit(solution)/shard_map/ppermute | solution.py:56
  809.6 56.8 %collective-permute-start.42 = (bf16[512,2048]{1,0:T(8,128)(2,1)}, bf16[512,2048]{1,0:T(8,128)(2,1)}, u32[]{:S(2)}, u32[]{:S(2)}) collective-permute-start(bf16[512,2048]{1,0:T(8,128)(2,1)} %get-tuple-element.394), channel_id=1, source_target_pairs={{1,0},{0,1},{3,2},{2,3},{5,4},{4,5},{7,6},{6,7},{9,8},{8,9},{11,10... | collective-permute-start | bytes 6291464 | tf_op jit(solution)/shard_map/ppermute | solution.py:46
  866.3 97.1 %reduce-scatter.20.cloned.1.call-start = ((), (), s32[]{:S(2)}) async-start(), calls=%async_computation.14 | async-start | bytes 737280 | tf_op jit(solution)/shard_map/reduce_scatter | solution.py:112
  944.3 48.1 %collective-permute-start.57 = (bf16[512,2048]{1,0:T(8,128)(2,1)}, bf16[512,2048]{1,0:T(8,128)(2,1)}, u32[]{:S(2)}, u32[]{:S(2)}) collective-permute-start(bf16[512,2048]{1,0:T(8,128)(2,1)} %fusion.14), channel_id=1, source_target_pairs={{2,0},{3,1},{0,2},{1,3},{6,4},{7,5},{4,6},{5,7},{10,8},{11,9},{8,1... | collective-permute-start | bytes 6291464 | tf_op jit(solution)/shard_map/ppermute | solution.py:46
  (162 other events, 2305.4 us)
Sparse Core Ops, SparseCore 0:
  36.7 38.3 all-gather.13
  88.8 46.7 all-gather.15
  137.7 44.6 all-gather.17
  184.4 44.6 all-gather.19
  231.1 44.6 all-gather.21
  321.8 79.3 all-gather.11
  529.0 75.1 reduce-scatter.13
  613.8 41.2 reduce-scatter.7
  693.0 41.9 reduce-scatter.9
  737.7 43.1 reduce-scatter.11
  798.2 42.5 reduce-scatter.17
  866.4 33.0 reduce-scatter.15
  943.2 20.1 reduce-scatter.19
